TPU v7x, 512 devices: a whole 4x8x8 slice. The times are simulated.
512 devices in a mesh: row: 32 (over z, x), col: 8 (over y), mat: 2 (over core).
Axes of the slice: x: 4, y: 8, z: 8, core: 2. Of those that a mesh axis runs over, the one named last changes fastest.
Arguments:
- weight: bfloat16 [2, 8192, 14336], P('mat', 'row', 'col'), may hold values from -6 to 6
- gradient: bfloat16 [2, 8192, 14336], P('mat', 'row', 'col'), may hold values from -600 to 600
- momentum: bfloat16 [2, 8192, 14336], P('mat', 'row', 'col'), may hold values from -6 to 6
- basis_in: float32 [2, 14336, 512], P('mat', ('col', 'row')), may hold values from -6 to 6
Outputs:
- new_weight: bfloat16 [2, 8192, 14336], P('mat', 'row', 'col')
- new_momentum: bfloat16 [2, 8192, 14336], P('mat', 'row', 'col')
- new_basis: float32 [2, 14336, 512], P('mat', ('col', 'row'))
All inputs are finite; a program needn't handle non-finite values.
Results may differ from a plain program's by a relative error of at most 0.006.
Values may be sent and summed in bfloat16 or wider, within the bound.
No kernel may reach another device: no remote copies, remote signals or barrier semaphores. Data moves between devices by JAX's collectives and lax.ppermute only.
A program may use at most 64 MiB of HBM per device.

v0:
```python
import math

import jax
import jax.numpy as jnp
from jax import lax
from jax.sharding import PartitionSpec as P

ROWS = 8192
COLS = 14336
RANK = 512


momentum_keep = 0.95
step_size = 0.25
epsilon = 1e-06


def orthonormal(summed):
    gram_matrix = lax.dot_general(
        summed, summed, (((0,), (0,)), ((), ())), precision=lax.Precision.HIGHEST
    )
    return gram_matrix


def on_device(weight, gradient, momentum, basis_in):
    weight_local = weight[0]
    grads = gradient[0].astype(jnp.float32)
    basis_low = basis_in[0].astype(jnp.bfloat16)
    square_total = lax.psum(jnp.sum(grads * grads), ("row", "col", "mat"))
    root_mean = jnp.sqrt(square_total / (2.0 * ROWS * COLS))
    clip_scale = 1.0 / jnp.maximum(1.0, root_mean)
    blend32 = momentum[0].astype(jnp.float32) + clip_scale * grads
    blended = blend32.astype(jnp.bfloat16)
    columns = blended
    partial_left = jnp.dot(
        columns,
        lax.all_gather(basis_low, "row", axis=0, tiled=True),
        preferred_element_type=jnp.float32,
    )
    summed = lax.psum(partial_left, "col")
    gram_matrix = lax.psum(orthonormal(summed), "row")
    chol_factor = jnp.linalg.cholesky(gram_matrix)
    ortho = jax.scipy.linalg.solve_triangular(chol_factor, summed.T, lower=True).T
    ortho_low = ortho.astype(jnp.bfloat16)
    columns = blended
    right_factor = lax.psum_scatter(
        lax.dot_general(
            columns, ortho_low, (((0,), (0,)), ((), ())), preferred_element_type=jnp.float32
        ),
        "row",
        scatter_dimension=0,
        tiled=True,
    )
    column_squares = lax.psum(jnp.sum(right_factor * right_factor, axis=0), ("row", "col"))
    inverse = math.sqrt(COLS) * lax.rsqrt(column_squares + epsilon)
    new_basis = right_factor * inverse
    factor = step_size * math.sqrt(ROWS / RANK)
    stretched = ortho / inverse
    block_piece = lax.all_gather(new_basis, "row", axis=0, tiled=True)
    update = lax.dot_general(
        ortho, block_piece, (((1,), (1,)), ((), ())), precision=lax.Precision.HIGHEST
    )
    feedback = lax.dot_general(
        stretched, block_piece, (((1,), (1,)), ((), ())), precision=lax.Precision.HIGHEST
    )
    products = jnp.stack((update, feedback))
    new_weight = (weight_local.astype(jnp.float32) - factor * products[0]).astype(jnp.bfloat16)
    new_momentum = (blend32 - (1.0 - momentum_keep) * products[1]).astype(jnp.bfloat16)
    return (new_weight[None], new_momentum[None], new_basis[None])


def solution(mesh):
    in_specs = (
        P("mat", "row", "col"),
        P("mat", "row", "col"),
        P("mat", "row", "col"),
        P("mat", ("col", "row"), None),
    )
    out_specs = (P("mat", "row", "col"), P("mat", "row", "col"), P("mat", ("col", "row"), None))
    return jax.shard_map(
        on_device, mesh=mesh, in_specs=in_specs, out_specs=out_specs, check_vma=False
    )
```

profile of v0, /device:TPU:6, one launch (start us, length us, event | category | flops | bytes accessed | tf_op | source)
XLA Modules:
  0.0 1518.8 jit_solution(15133164528957215646)
XLA Ops:
  7.2 0.0 all-gather.6.cloned.1.call-start
  7.2 1.5 convert_element_type.38
  8.7 0.0 all-gather.6.cloned.1.call-update
  8.8 0.0 all-reduce.4.cloned.1.call-start
  8.8 2.3 fusion.5
  11.1 104.2 %psum.28 = f32[]{:T(128)} all-reduce(f32[]{:T(128)} %fusion.5), channel_id=1, replica_groups=mesh['row'=32,'col'=8,'mat'=2] {'row','col','mat'}, use_global_device_ids=true, to_apply=%region_1.0 | all-reduce | flops 1 | bytes 8 | tf_op jit(solution)/shard_map/psum | solution.py:29
  116.1 0.0 all-gather.6.cloned.1.call-done
  116.1 3.5 fusion.8
  119.6 0.0 all-reduce.6.cloned.1.call-start
  119.7 75.0 %all-reduce.4.cloned.1.call-done = f32[256,512]{1,0:T(8,128)} async-done(((f32[256,512]{1,0:T(8,128)}), f32[256,512]{1,0:T(8,128)}) %all-reduce.4.cloned.1.call-update) | async-done | bytes 524304 | tf_op jit(solution)/shard_map/psum | solution.py:40
  194.7 3.3 fusion.51
  198.0 0.2 reduce-scatter.2.cloned.1.call-start
  198.2 158.5 %all-reduce.6.cloned.1.call-done = f32[512,512]{0,1:T(8,128)} async-done(((f32[512,512]{0,1:T(8,128)}), f32[512,512]{0,1:T(8,128)}) %all-reduce.6.cloned.1.call-update) | async-done | bytes 1048592 | tf_op jit(solution)/shard_map/psum | solution.py:41
  356.7 1.6 copy.8
  358.4 0.2 fusion.11
  358.7 11.7 cholesky.104
  370.4 9.8 custom-call.31
  380.2 0.1 cholesky.224
  380.3 0.3 constant_dynamic-update-slice_fusion.3
  380.7 0.3 convolution_subtract_fusion.1
  381.0 11.7 cholesky.217
  392.8 10.2 custom-call.32
  403.0 0.3 convolution_dynamic-update-slice_fusion
  403.2 0.4 convolution_subtract_fusion.4
  403.6 11.7 cholesky.238
  415.4 0.7 compare_reduce_fusion.1
  416.1 9.8 custom-call.33
  425.9 0.2 convolution_dynamic-update-slice_fusion.1
  426.1 0.4 convolution_subtract_fusion.6
  426.5 11.7 cholesky.255
  438.3 0.6 compare_reduce_fusion
  438.9 0.6 compare_reduce_fusion.2
  442.1 1.3 select_select_fusion
  443.4 11.6 while.1
  443.4 0.1 constant_dynamic-slice_fusion.2
  443.4 0.5 fusion.63
  444.0 2.3 bitcast_dynamic-update-slice_fusion.2
  446.3 0.1 constant_dynamic-slice_fusion.2
  446.4 0.5 fusion.63
  446.9 2.3 bitcast_dynamic-update-slice_fusion.2
  449.2 0.1 constant_dynamic-slice_fusion.2
  449.3 0.5 fusion.63
  449.8 2.3 bitcast_dynamic-update-slice_fusion.2
  452.1 0.1 constant_dynamic-slice_fusion.2
  452.2 0.5 fusion.63
  452.7 2.2 bitcast_dynamic-update-slice_fusion.2
  455.0 39.3 %custom-call.34 = f32[4,128,128]{1,2,0:T(8,128)S(1)} custom-call(f32[4,128,128]{2,1,0:T(8,128)S(1)} %get-tuple-element.10), custom_call_target="InvertDiagBlocksLowerTriangular" | custom-call | tf_op jit(solution)/shard_map/jit(_solve_triangular)/triangular_solve | solution.py:43
  494.3 0.3 fusion.32
  494.6 1.2 convolution_subtract_fusion.5
  495.8 0.3 fusion.39
  496.2 1.5 convolution_subtract_fusion.3
  497.7 0.3 fusion.37
  498.0 1.7 convolution_subtract_fusion.2
  499.7 0.3 fusion.36
  500.1 2.5 fusion.23
  502.6 0.0 all-gather.4.cloned.1.call-start
  502.6 224.8 %reduce-scatter.2.cloned.1.call-done = f32[56,512]{1,0:T(8,128)} async-done(((f32[1792,512]{1,0:T(8,128)}), f32[56,512]{1,0:T(8,128)}) %reduce-scatter.2.cloned.1.call-update) | async-done | bytes 114704 | tf_op jit(solution)/shard_map/reduce_scatter | solution.py:46
  727.4 0.9 multiply_reduce_fusion
  728.3 627.4 %psum.31 = f32[512]{0:T(512)S(1)} all-reduce(f32[512]{0:T(512)S(1)} %multiply_reduce_fusion), channel_id=1, replica_groups=mesh['row'=32,'col'=8,'mat'=2] {'row','col'}, use_global_device_ids=true, to_apply=%region_14.15 | all-reduce | flops 512 | bytes 4096 | tf_op jit(solution)/shard_map/psum | solution.py:54
  1355.7 1.6 broadcast_multiply_fusion
  1357.3 1.6 fusion.61
  1358.9 137.1 %all-gather.4.cloned.1.call-done = f32[1792,512]{1,0:T(8,128)} async-done(((f32[56,512]{1,0:T(8,128)}), f32[1792,512]{1,0:T(8,128)}) %all-gather.4.cloned.1.call-update) | async-done | bytes 3670032 | tf_op jit(solution)/shard_map/all_gather | solution.py:59
  1496.0 9.2 fusion.3
  1505.2 6.9 fusion.4
  (27 shorter events, 0.3 us)
Async XLA Ops:
  7.2 108.9 %all-gather.6.cloned.1.call-start = ((), (), s32[]{:S(2)}) async-start(), calls=%async_computation.5 | async-start | bytes 1892352 | tf_op jit(solution)/shard_map/all_gather | solution.py:37
  8.8 185.9 %all-reduce.4.cloned.1.call-start = ((), (), s32[]{:S(2)}) async-start(), calls=%async_computation.1 | async-start | bytes 1048576 | tf_op jit(solution)/shard_map/psum | solution.py:40
  119.6 237.1 %all-reduce.6.cloned.1.call-start = ((), (), s32[]{:S(2)}) async-start(), calls=%async_computation.2 | async-start | bytes 2097152 | tf_op jit(solution)/shard_map/psum | solution.py:41
  198.0 529.4 %reduce-scatter.2.cloned.1.call-start = ((), (), s32[]{:S(2)}) async-start(), calls=%async_computation.3 | async-start | bytes 3784704 | tf_op jit(solution)/shard_map/reduce_scatter | solution.py:46
  356.7 1.7 copy-start.3
  415.4 78.9 %copy-start.2 = (f32[256,512]{1,0:T(8,128)S(1)}, f32[256,512]{1,0:T(8,128)}, u32[]{:S(2)}) copy-start(f32[256,512]{1,0:T(8,128)} %all-reduce.4.cloned.1.call-done) | copy-start | bytes 1572868
  454.9 45.1 %copy-start.1 = (bf16[1,256,1792]{2,1,0:T(8,128)(2,1)S(1)}, bf16[1,256,1792]{2,1,0:T(8,128)(2,1)}, u32[]{:S(2)}) copy-start(bf16[1,256,1792]{2,1,0:T(8,128)(2,1)} %param.5) | copy-start | bytes 2752516
  454.9 45.1 %copy-start.4 = (bf16[1,256,1792]{2,1,0:T(8,128)(2,1)S(1)}, bf16[1,256,1792]{2,1,0:T(8,128)(2,1)}, u32[]{:S(2)}) copy-start(bf16[1,256,1792]{2,1,0:T(8,128)(2,1)} %param.6) | copy-start | bytes 2752516
  502.6 993.4 %all-gather.4.cloned.1.call-start = ((), (), s32[]{:S(2)}) async-start(), calls=%async_computation.4 | async-start | bytes 3784704 | tf_op jit(solution)/shard_map/all_gather | solution.py:59
  1496.0 9.2 copy-start
  1496.0 9.2 copy-start.5
Sparse Core Ops, SparseCore 0:
  11.7 87.2 all-gather.5
  119.7 74.8 all-reduce.3
  198.5 158.1 all-reduce.5
  502.7 224.6 reduce-scatter.1
  1357.4 138.5 all-gather.3
where the time goes:
time: 1520 us
  blocking collectives  732 us (48%)
  waiting for transfers between devices  596 us (39%)
  other arithmetic  127 us (8%)
  matrix products  33 us (2%)
  between operations  17.5 us (1%)
    psum x1, blocking collectives, on_device(): lax.psum(jnp.sum(right_factor * right_factor, axis=0), ('row', 'col'))  627 us
    reduce_scatter x1, waiting for transfers between devices, on_device(): lax.psum_scatter(lax.dot_general(columns, ortho_low, (((0,), (0,)), ((),...  225 us
    psum x1, waiting for transfers between devices, on_device(): gram_matrix = lax.psum(orthonormal(summed), 'row')  158 us
    all_gather x1, waiting for transfers between devices, on_device(): block_piece = lax.all_gather(new_basis, 'row', axis=0, tiled=True)  137 us
    psum x1, blocking collectives, on_device(): square_total = lax.psum(jnp.sum(grads * grads), ('row', 'col', 'mat'))  104 us
    another operation x14, other arithmetic, on_device(): chol_factor = jnp.linalg.cholesky(gram_matrix)  78.8 us
    psum x1, waiting for transfers between devices, on_device(): summed = lax.psum(partial_left, 'col')  75 us
    another operation x3, other arithmetic, on_device(): jax.scipy.linalg.solve_triangular(chol_factor, summed.T, lower=True)  40.6 us
  transfers between devices with their start and end apart: 5, of which 4 were waited for; matrix products, arithmetic and copies ran while one was open for 0% of the time, Pallas kernels for 0%

commit v1 on v0

v1 whole, which is shorter than its diff:
```python
import functools
import math

import jax
import jax.numpy as jnp
from jax import lax
from jax.experimental import pallas as pl
from jax.experimental.pallas import tpu as pltpu
from jax.sharding import Mesh
from jax.sharding import PartitionSpec as P

ROWS = 8192
COLS = 14336
RANK = 512
BLOCK = 128
PIVOTS = 8

momentum_keep = 0.95
step_size = 0.25
epsilon = 1e-06

f32 = jnp.float32
bf16 = jnp.bfloat16
HIGHEST = lax.Precision.HIGHEST
TN = (((0,), (0,)), ((), ()))
NT = (((1,), (1,)), ((), ()))


def block_inverse(block):
    tiles = BLOCK // 8
    full = (8, BLOCK)
    work = [block[8 * v : 8 * v + 8, :] for v in range(tiles)]
    row = lax.broadcasted_iota(jnp.int32, full, 0)
    lane = lax.broadcasted_iota(jnp.int32, full, 1)
    inverse = [jnp.where(lane == row + 8 * v, 1.0, 0.0).astype(f32) for v in range(tiles)]
    scale = [None] * tiles

    def across(tile, j):
        return jnp.broadcast_to(tile[:, j : j + 1], full)

    def down(tile, s):
        return jnp.broadcast_to(tile[s : s + 1, :], full)

    for j in range(0, BLOCK, PIVOTS):
        at, s = divmod(j, 8)
        first = [across(work[at], j + a) for a in range(PIVOTS)]
        pivot = [[down(first[b], s + a) for b in range(a + 1)] for a in range(PIVOTS)]
        rows = [down(work[at], s + a) for a in range(PIVOTS)]
        rows_inv = [down(inverse[at], s + a) for a in range(PIVOTS)]
        lower = [[None] * PIVOTS for _ in range(PIVOTS)]
        recip = [None] * PIVOTS
        for a in range(PIVOTS):
            recip[a] = 1.0 / pivot[a][a]
            root = lax.rsqrt(pivot[a][a])
            scale[at] = root if s + a == 0 else jnp.where(row >= s + a, root, scale[at])
            for i in range(a + 1, PIVOTS):
                lower[i][a] = pivot[i][a] * recip[a]
                for b in range(a + 1, i + 1):
                    pivot[i][b] = pivot[i][b] - lower[i][a] * pivot[b][a]
                rows[i] = rows[i] - lower[i][a] * rows[a]
                rows_inv[i] = rows_inv[i] - lower[i][a] * rows_inv[a]
        unit = [rows[a] * recip[a] for a in range(PIVOTS)]
        unit_inv = [rows_inv[a] * recip[a] for a in range(PIVOTS)]
        for v in range(at, tiles):
            column = first if v == at else [across(work[v], j + a) for a in range(PIVOTS)]
            column = list(column)
            for a in range(PIVOTS):
                for i in range(a + 1, PIVOTS):
                    column[i] = column[i] - lower[i][a] * column[a]
            for a in range(PIVOTS):
                factor = column[a]
                if v == at:
                    if s + a == 7:
                        continue
                    factor = jnp.where(row > s + a, factor, 0.0)
                if not (v == at and s + PIVOTS == 8):
                    work[v] = work[v] - factor * unit[a]
                inverse[v] = inverse[v] - factor * unit_inv[a]
    return jnp.concatenate([inverse[v] * scale[v] for v in range(tiles)], axis=0)


def chol_inverse_kernel(gram_ref, out_ref, work_ref):
    work_ref[:, :RANK] = gram_ref[...]
    i = lax.broadcasted_iota(jnp.int32, (RANK, RANK), 0)
    j = lax.broadcasted_iota(jnp.int32, (RANK, RANK), 1)
    work_ref[:, RANK:] = jnp.where(i == j, 1.0, 0.0).astype(f32)
    for k in range(0, RANK, BLOCK):
        end = k + BLOCK
        left = RANK - end
        inverse = block_inverse(work_ref[k:end, k:end])
        wide = jnp.dot(
            inverse, work_ref[k:end, end : RANK + end], precision=HIGHEST, preferred_element_type=f32
        )
        out_ref[k:end, :end] = wide[:, left:]
        if left:
            out_ref[k:end, end:] = jnp.zeros((BLOCK, left), f32)
            work_ref[end:, end : RANK + end] = work_ref[end:, end : RANK + end] - lax.dot_general(
                wide[:, :left], wide, TN, precision=HIGHEST, preferred_element_type=f32
            )


def chol_inverse(gram):
    return pl.pallas_call(
        chol_inverse_kernel,
        out_shape=jax.ShapeDtypeStruct((RANK, RANK), f32),
        in_specs=[pl.BlockSpec(memory_space=pltpu.VMEM)],
        out_specs=pl.BlockSpec(memory_space=pltpu.VMEM),
        scratch_shapes=[pltpu.VMEM((RANK, 2 * RANK), f32)],
        compiler_params=pltpu.CompilerParams(vmem_limit_bytes=16 * 2**20),
        cost_estimate=pl.CostEstimate(flops=2 * 10**9, bytes_accessed=2 * 2**20, transcendentals=0),
        name="chol_inverse",
    )(gram)


def swap_sum(x, axis, dim):
    return jnp.sum(lax.all_to_all(x, axis, dim, dim, tiled=True), axis=dim)


def spread_sum(x, axis, size):
    return swap_sum(jnp.broadcast_to(x[None], (size,) + x.shape), axis, 0)


def on_device(weight, gradient, momentum, basis_in):
    weight_local = weight[0]
    grads = gradient[0].astype(f32)
    basis_low = basis_in[0].astype(bf16)
    basis_x = lax.all_gather(basis_low, "x", axis=0, tiled=True)
    basis_all = lax.all_gather(basis_x, "z", axis=0, tiled=True)

    squares = jnp.full((1, 128), jnp.sum(grads * grads), f32)
    squares = spread_sum(squares, ("z", "x"), 32)
    squares = spread_sum(squares, "y", 8)
    square_total = lax.psum(squares[0, 0], "core")
    root_mean = jnp.sqrt(square_total / (2.0 * ROWS * COLS))
    clip_scale = 1.0 / jnp.maximum(1.0, root_mean)
    blend32 = momentum[0].astype(f32) + clip_scale * grads
    blended = blend32.astype(bf16)

    partial_left = jnp.dot(blended, basis_all, preferred_element_type=f32)
    left_rows = swap_sum(partial_left.reshape(8, 32, RANK), "y", 0)
    left = lax.all_gather(left_rows, "y", axis=0, tiled=True)

    gram_part = lax.dot_general(left, left, TN, precision=HIGHEST)
    gram_part = lax.dynamic_slice_in_dim(gram_part, lax.axis_index("y") * 64, 64, axis=0)
    gram_rows = swap_sum(gram_part.reshape(4, 16, RANK), "x", 0)
    gram_rows = spread_sum(gram_rows, "z", 8)
    gram_rows = lax.all_gather(gram_rows, "x", axis=0, tiled=True)
    gram_matrix = lax.all_gather(gram_rows, "y", axis=0, tiled=True)

    high = lax.reduce_precision(left, 8, 7)
    low = (left - high).astype(bf16)
    high = high.astype(bf16)
    product = lax.dot_general(blended, high, TN, preferred_element_type=f32)
    product = product + lax.dot_general(blended, low, TN, preferred_element_type=f32)
    product = swap_sum(product.reshape(8, 4, 56, RANK), "x", 1)
    product = swap_sum(product, "z", 0)
    product_all = lax.all_gather(product.astype(bf16), "x", axis=0, tiled=True)
    product_all = lax.all_gather(product_all, "z", axis=0, tiled=True)

    inverse_factor = chol_inverse(gram_matrix)
    ortho = lax.dot_general(left, inverse_factor, NT, precision=HIGHEST)
    right_own = lax.dot_general(product, inverse_factor, NT, precision=HIGHEST)
    right_all = lax.dot_general(product_all.astype(f32), inverse_factor, NT, precision=HIGHEST)

    column_squares = spread_sum(jnp.sum(right_all * right_all, axis=0, keepdims=True), "y", 8)
    right_low = right_all.astype(bf16)
    feedback = lax.dot_general(ortho.astype(bf16), right_low, NT, preferred_element_type=f32)
    new_momentum = (blend32 - (1.0 - momentum_keep) * feedback).astype(bf16)
    stretch = math.sqrt(COLS) * lax.rsqrt(column_squares + epsilon)
    new_basis = right_own * stretch
    factor = step_size * math.sqrt(ROWS / RANK)
    update = lax.dot_general(
        (ortho * stretch).astype(bf16), right_low, NT, preferred_element_type=f32
    )
    new_weight = (weight_local.astype(f32) - factor * update).astype(bf16)
    return (new_weight[None], new_momentum[None], new_basis[None])


def solution(mesh):
    devices = mesh.devices.reshape(8, 4, 8, 2)
    fine = Mesh(devices, ("z", "x", "y", "core"))
    matrix = P("core", ("z", "x"), "y")
    basis = P("core", ("y", "z", "x"), None)
    return jax.shard_map(
        on_device,
        mesh=fine,
        in_specs=(matrix, matrix, matrix, basis),
        out_specs=(matrix, matrix, basis),
        check_vma=False,
    )
```

time: 1520 us -> 298 us (0.20)
  blocking collectives: 732 us -> 145 us
  waiting for transfers between devices: 596 us -> 47.8 us
  other arithmetic: 127 us -> 8.65 us
  starting transfers between devices: 0.38 us -> 29.4 us
  Pallas kernels: 0 us -> 20.7 us
    psum x2 -> x1, blocking collectives: 732 us -> 2.96 us  [on_device(): square_total = lax.psum(squares[0, 0], 'core')]
    psum x2 -> x0, waiting for transfers between devices: 234 us -> none  [the longest x1 158 us: on_device(): gram_matrix = lax.psum(orthonormal(summed), 'row')]
    reduce_scatter x1 -> x0, waiting for transfers between devices: 225 us -> none  [on_device(): lax.psum_scatter(lax.dot_general(columns, ortho_low, (((0,), (0,)), ((),...]
    another operation x17 -> x0, other arithmetic: 119 us -> none  [the longest x14 78.8 us: on_device(): chol_factor = jnp.linalg.cholesky(gram_matrix)]
    all_gather x2 -> x3, waiting for transfers between devices: 137 us -> 22.3 us  [the longest x1 17.4 us: on_device(): product_all = lax.all_gather(product_all, 'z', axis=0, tiled=True)]
    all_gather x0 -> x4, blocking collectives: none -> 88 us  [the longest x1 34.1 us: on_device(): gram_rows = lax.all_gather(gram_rows, 'x', axis=0, tiled=True)]
    all_to_all x0 -> x3, blocking collectives: none -> 53.6 us  [swap_sum(): return jnp.sum(lax.all_to_all(x, axis, dim, dim, tiled=True), axis=dim)]
    all_to_all x0 -> x5, starting transfers between devices: none -> 29.3 us  [swap_sum(): return jnp.sum(lax.all_to_all(x, axis, dim, dim, tiled=True), axis=dim)]
  transfers between devices with their start and end apart: 5 -> 8, of which waited for: 4 -> 6; matrix products, arithmetic and copies ran while one was open for 0% -> 7% of each run, Pallas kernels for 0% -> 7%
where the time goes in v1:
time: 298 us; the launch traced here: 297 us
  blocking collectives  145 us (49%)
  waiting for transfers between devices  47.8 us (16%)
  starting transfers between devices  29.4 us (10%)
  matrix products  24.8 us (8%)
  Pallas kernels  20.7 us (7%)
  between operations  14.6 us (5%)
  other arithmetic  8.65 us (3%)
  local copies, waits for them, and re-layouts  6.15 us (2%)
    all_to_all x3, blocking collectives, swap_sum(): return jnp.sum(lax.all_to_all(x, axis, dim, dim, tiled=True), axis=dim)  53.6 us
    all_gather x1, blocking collectives, on_device(): gram_rows = lax.all_gather(gram_rows, 'x', axis=0, tiled=True)  34.1 us
    all_to_all x5, starting transfers between devices, swap_sum(): return jnp.sum(lax.all_to_all(x, axis, dim, dim, tiled=True), axis=dim)  29.3 us
    all_to_all x5, waiting for transfers between devices, swap_sum(): return jnp.sum(lax.all_to_all(x, axis, dim, dim, tiled=True), axis=dim)  25.5 us
    all_gather x1, blocking collectives, on_device(): left = lax.all_gather(left_rows, 'y', axis=0, tiled=True)  25.2 us
    pallas_call x1, Pallas kernels, chol_inverse(): pl.pallas_call(chol_inverse_kernel, out_shape=jax.ShapeDtypeStruct((RANK,...  20.7 us
    all_gather x1, waiting for transfers between devices, on_device(): product_all = lax.all_gather(product_all, 'z', axis=0, tiled=True)  17.4 us
    all_gather x1, blocking collectives, on_device(): basis_x = lax.all_gather(basis_low, 'x', axis=0, tiled=True)  15.6 us
  transfers between devices with their start and end apart: 8, of which 6 were waited for; matrix products, arithmetic and copies ran while one was open for 7% of the time, Pallas kernels for 7%

profile of v1, /device:TPU:6, one launch (start us, length us, event | category | flops | bytes accessed | tf_op | source)
XLA Modules:
  0.0 296.8 jit_solution(8957471090207850059)
XLA Ops:
  7.2 0.0 copy-start.1
  7.2 0.0 all-gather.10.cloned.1.call-start
  7.2 1.0 convert_element_type.64
  8.2 15.6 %all-gather = bf16[1,224,512]{2,1,0:T(8,128)(2,1)} all-gather(bf16[1,56,512]{2,1,0:T(8,128)(2,1)S(1)} %convert_element_type.64), channel_id=2, replica_groups=mesh['z'=8,'x'=4,'y'=8,'core'=2] {'x'}, dimensions={1}, use_global_device_ids=true | all-gather | bytes 286720 | tf_op jit(solution)/shard_map/all_gather | solution.py:127
  23.8 0.0 all-gather.10.cloned.1.call-update
  23.8 2.3 fusion.5
  26.0 0.7 broadcast_in_dim_broadcast_in_dim_broadcast_in_dim.3
  26.7 18.5 %all_to_all.40 = f32[32,1,128]{2,1,0:T(1,128)S(1)} all-to-all(f32[32,1,128]{2,1,0:T(1,128)S(1)} %broadcast_in_dim_broadcast_in_dim_broadcast_in_dim.3), channel_id=1, replica_groups=mesh['z'=8,'x'=4,'y'=8,'core'=2] {'z','x'}, dimensions={0} | all-to-all | bytes 32768 | tf_op jit(solution)/shard_map/all_to_all | solution.py:116
  45.2 14.6 %all_to_all.41 = f32[8,1,128]{2,1,0:T(1,128)S(1)} all-to-all(f32[8,1,128]{2,1,0:T(1,128)S(1)} %broadcast_in_dim.12), channel_id=1, replica_groups=mesh['z'=8,'x'=4,'y'=8,'core'=2] {'y'}, dimensions={0} | all-to-all | bytes 8192 | tf_op jit(solution)/shard_map/all_to_all | solution.py:116
  59.8 3.0 psum.7
  63.5 0.0 copy-done.1
  63.5 1.5 fusion.9
  65.0 4.9 %all-gather.10.cloned.1.call-done = bf16[1,1792,512]{2,1,0:T(8,128)(2,1)} async-done(((bf16[1,224,512]{2,1,0:T(8,128)(2,1)}), bf16[1,1792,512]{2,1,0:T(8,128)(2,1)}) %all-gather.10.cloned.1.call-update) | async-done | bytes 1835024 | tf_op jit(solution)/shard_map/all_gather | solution.py:128
  69.9 2.9 fusion.7
  72.8 6.7 %all-to-all-start.2 = ((f32[8,32,512]{2,1,0:T(8,128)}), f32[8,32,512]{2,1,0:T(8,128)S(1)}, u32[]{:S(2)}, u32[]{:S(2)}) async-start(f32[8,32,512]{2,1,0:T(8,128)} %fusion.7), calls=%async_computation.2 | async-start | bytes 1048576 | tf_op jit(solution)/shard_map/all_to_all | solution.py:116
  79.4 0.0 copy-start.2
  79.4 13.9 %all-to-all-done.2 = f32[8,32,512]{2,1,0:T(8,128)S(1)} async-done(((f32[8,32,512]{2,1,0:T(8,128)}), f32[8,32,512]{2,1,0:T(8,128)S(1)}, u32[]{:S(2)}, u32[]{:S(2)}) %all-to-all-start.2) | async-done | bytes 524320 | tf_op jit(solution)/shard_map/all_to_all | solution.py:116
  93.4 25.2 %all_gather.23 = f32[256,512]{1,0:T(8,128)S(1)} all-gather(f32[32,512]{1,0:T(8,128)S(1)} %reduce_sum.96), channel_id=1, replica_groups=mesh['z'=8,'x'=4,'y'=8,'core'=2] {'y'}, dimensions={0}, use_global_device_ids=true | all-gather | bytes 589824 | tf_op jit(solution)/shard_map/all_gather | solution.py:141
  118.6 1.0 fusion.18
  119.7 0.7 constant_dynamic-slice_fusion
  120.3 4.8 %all-to-all-start.3 = ((f32[4,16,512]{2,1,0:T(8,128)}), f32[4,16,512]{2,1,0:T(8,128)S(1)}, u32[]{:S(2)}, u32[]{:S(2)}) async-start(f32[4,16,512]{2,1,0:T(8,128)} %bitcast.8), calls=%async_computation.3 | async-start | bytes 262144 | tf_op jit(solution)/shard_map/all_to_all | solution.py:116
  125.1 0.0 copy-done.2
  125.1 2.5 fusion.15
  127.6 1.4 all-to-all-done.3
  129.1 0.7 broadcast_in_dim.13
  129.8 4.4 %all-to-all-start.4 = ((f32[8,16,512]{2,1,0:T(8,128)}), f32[8,16,512]{2,1,0:T(8,128)S(1)}, u32[]{:S(2)}, u32[]{:S(2)}) async-start(f32[8,16,512]{2,1,0:T(8,128)} %broadcast_in_dim.13), calls=%async_computation.4 | async-start | bytes 524288 | tf_op jit(solution)/shard_map/all_to_all | solution.py:116
  134.2 2.7 convolution_add_fusion
  136.9 2.2 copy.11
  139.2 5.5 %all-to-all-done.4 = f32[8,16,512]{2,1,0:T(8,128)S(1)} async-done(((f32[8,16,512]{2,1,0:T(8,128)}), f32[8,16,512]{2,1,0:T(8,128)S(1)}, u32[]{:S(2)}, u32[]{:S(2)}) %all-to-all-start.4) | async-done | bytes 262176 | tf_op jit(solution)/shard_map/all_to_all | solution.py:116
  144.7 6.8 %all-to-all-start.5 = ((f32[8,4,56,512]{3,2,0,1:T(8,128)}), f32[8,4,56,512]{3,2,0,1:T(8,128)}, u32[]{:S(2)}, u32[]{:S(2)}) async-start(f32[8,4,56,512]{3,2,0,1:T(8,128)} %copy.11), calls=%async_computation.5 | async-start | bytes 7340032 | tf_op jit(solution)/shard_map/all_to_all | solution.py:116
  151.4 0.0 all-gather.6.cloned.1.call-start
  151.5 34.1 %all_gather.24 = f32[64,512]{1,0:T(8,128)} all-gather(f32[16,512]{1,0:T(8,128)S(1)} %reduce_sum.98), channel_id=1, replica_groups=mesh['z'=8,'x'=4,'y'=8,'core'=2] {'x'}, dimensions={0}, use_global_device_ids=true | all-gather | bytes 163840 | tf_op jit(solution)/shard_map/all_gather | solution.py:147
  185.5 0.0 all-gather.6.cloned.1.call-update
  185.6 0.0 all-gather.8.cloned.1.call-start
  185.6 0.0 all-to-all-done.5
  185.6 2.6 reduce_sum.99
  188.2 20.6 %all_to_all.42 = f32[8,56,512]{2,1,0:T(8,128)} all-to-all(f32[8,56,512]{2,1,0:T(8,128)S(1)} %reduce_sum.99), channel_id=1, replica_groups=mesh['z'=8,'x'=4,'y'=8,'core'=2] {'z'}, dimensions={0} | all-to-all | bytes 1835008 | tf_op jit(solution)/shard_map/all_to_all | solution.py:116
  208.8 1.3 reduce_sum.100
  210.1 13.1 %all_gather.26 = bf16[224,512]{1,0:T(8,128)(2,1)} all-gather(bf16[56,512]{1,0:T(8,128)(2,1)S(1)} %convert_element_type.69), channel_id=1, replica_groups=mesh['z'=8,'x'=4,'y'=8,'core'=2] {'x'}, dimensions={0}, use_global_device_ids=true | all-gather | bytes 286720 | tf_op jit(solution)/shard_map/all_gather | solution.py:157
  223.2 0.0 all-gather.8.cloned.1.call-update
  223.2 0.0 all-gather.6.cloned.1.call-done.gram_ref
  223.2 0.0 copy-start
  223.2 1.2 copy-done
  224.5 20.7 %chol_inverse.1 = f32[512,512]{1,0:T(8,128)S(1)} custom-call(f32[512,512]{1,0:T(8,128)S(1)} %copy-done), custom_call_target="tpu_custom_call" | custom-call | flops 2000000000 | bytes 2097152 | tf_op jit(solution)/shard_map/chol_inverse/pallas_call | solution.py:103
  245.2 1.9 fusion.19
  247.0 0.0 copy-start.3
  247.0 17.4 %all-gather.8.cloned.1.call-done = bf16[1792,512]{1,0:T(8,128)(2,1)} async-done(((bf16[224,512]{1,0:T(8,128)(2,1)}), bf16[1792,512]{1,0:T(8,128)(2,1)}) %all-gather.8.cloned.1.call-update) | async-done | bytes 1835024 | tf_op jit(solution)/shard_map/all_gather | solution.py:158
  264.4 5.8 %multiply_reduce_fusion = (f32[512]{0:T(512)S(1)}, bf16[1792,512]{1,0:T(8,128)(2,1)}) fusion(bf16[1792,512]{1,0:T(8,128)(2,1)} %all-gather.8.cloned.1.call-done, f32[512,512]{1,0:T(8,128)S(1)} %chol_inverse.1), kind=kOutput, calls=%fused_computation | convolution fusion | flops 5639896576 | bytes 4720640 | tf_op jit(solution)/shard_map/dot_general | solution.py:163
  270.3 0.6 broadcast_in_dim.28
  270.9 6.7 %all-to-all-start.7 = ((f32[8,1,512]{2,1,0:T(1,128)}), f32[8,1,512]{2,1,0:T(1,128)S(1)}, u32[]{:S(2)}, u32[]{:S(2)}) async-start(f32[8,1,512]{2,1,0:T(1,128)} %broadcast_in_dim.28), calls=%async_computation.7 | async-start | bytes 32768 | tf_op jit(solution)/shard_map/all_to_all | solution.py:116
  277.6 0.0 copy-done.3
  277.6 3.1 %fusion.4 = bf16[1,256,1792]{2,1,0:T(8,128)(2,1)} fusion(bf16[1,256,1792]{2,1,0:T(8,128)(2,1)S(1)} %copy-done.1, bf16[1,256,1792]{2,1,0:T(8,128)(2,1)S(1)} %copy-done.2, bf16[1792,512]{1,0:T(8,128)(2,1)} %get-tuple-element.4, f32[]{:T(128)S(6)} %div.7, f32[256,512]{1,0:T(8,128)S(1)} %copy-done.3), kind=kOutput, calls=%fused_computation.8 | convolution fusion | flops 473104384 | bytes 5111812 | tf_op jit(solution)/shard_map/dot_general | solution.py:167
  280.7 0.0 copy-start.4
  280.7 4.7 %all-to-all-done.7 = f32[8,1,512]{2,1,0:T(1,128)S(1)} async-done(((f32[8,1,512]{2,1,0:T(1,128)}), f32[8,1,512]{2,1,0:T(1,128)S(1)}, u32[]{:S(2)}, u32[]{:S(2)}) %all-to-all-start.7) | async-done | bytes 16416 | tf_op jit(solution)/shard_map/all_to_all | solution.py:116
  285.4 1.8 fusion.10
  287.1 0.0 copy-done.4
  287.1 3.1 %fusion.3 = bf16[1,256,1792]{2,1,0:T(8,128)(2,1)} fusion(bf16[1,256,1792]{2,1,0:T(8,128)(2,1)S(1)} %copy-done.4, bf16[1792,512]{1,0:T(8,128)(2,1)} %get-tuple-element.4, f32[256,512]{1,0:T(8,128)S(1)} %copy-done.3, f32[512]{0:T(512)S(1)} %rsqrt_multiply_fusion), kind=kOutput, calls=%fused_computation.7 | convolution fusion | flops 471400448 | bytes 4196352 | tf_op jit(solution)/shard_map/dot_general | solution.py:172
  (9 shorter events, 0.2 us)
Async XLA Ops:
  7.2 56.3 %copy-start.1 = (bf16[1,256,1792]{2,1,0:T(8,128)(2,1)S(1)}, bf16[1,256,1792]{2,1,0:T(8,128)(2,1)}, u32[]{:S(2)}) copy-start(bf16[1,256,1792]{2,1,0:T(8,128)(2,1)} %param.5) | copy-start | bytes 2752516
  7.2 62.7 %all-gather.10.cloned.1.call-start = ((), (), s32[]{:S(2)}) async-start(), calls=%async_computation.10 | async-start | bytes 2064384 | tf_op jit(solution)/shard_map/all_gather | solution.py:128
  72.8 20.6 %all-to-all-start.2 = ((f32[8,32,512]{2,1,0:T(8,128)}), f32[8,32,512]{2,1,0:T(8,128)S(1)}, u32[]{:S(2)}, u32[]{:S(2)}) async-start(f32[8,32,512]{2,1,0:T(8,128)} %fusion.7), calls=%async_computation.2 | async-start | bytes 1048576 | tf_op jit(solution)/shard_map/all_to_all | solution.py:116
  79.4 45.7 %copy-start.2 = (bf16[1,256,1792]{2,1,0:T(8,128)(2,1)S(1)}, bf16[1,256,1792]{2,1,0:T(8,128)(2,1)}, u32[]{:S(2)}) copy-start(bf16[1,256,1792]{2,1,0:T(8,128)(2,1)} %param.6) | copy-start | bytes 2752516
  120.3 8.7 %all-to-all-start.3 = ((f32[4,16,512]{2,1,0:T(8,128)}), f32[4,16,512]{2,1,0:T(8,128)S(1)}, u32[]{:S(2)}, u32[]{:S(2)}) async-start(f32[4,16,512]{2,1,0:T(8,128)} %bitcast.8), calls=%async_computation.3 | async-start | bytes 262144 | tf_op jit(solution)/shard_map/all_to_all | solution.py:116
  129.8 14.9 %all-to-all-start.4 = ((f32[8,16,512]{2,1,0:T(8,128)}), f32[8,16,512]{2,1,0:T(8,128)S(1)}, u32[]{:S(2)}, u32[]{:S(2)}) async-start(f32[8,16,512]{2,1,0:T(8,128)} %broadcast_in_dim.13), calls=%async_computation.4 | async-start | bytes 524288 | tf_op jit(solution)/shard_map/all_to_all | solution.py:116
  144.7 41.0 %all-to-all-start.5 = ((f32[8,4,56,512]{3,2,0,1:T(8,128)}), f32[8,4,56,512]{3,2,0,1:T(8,128)}, u32[]{:S(2)}, u32[]{:S(2)}) async-start(f32[8,4,56,512]{3,2,0,1:T(8,128)} %copy.11), calls=%async_computation.5 | async-start | bytes 7340032 | tf_op jit(solution)/shard_map/all_to_all | solution.py:116
  151.4 71.8 %all-gather.6.cloned.1.call-start = ((), (), s32[]{:S(2)}) async-start(), calls=%async_computation.8 | async-start | bytes 1179648 | tf_op jit(solution)/shard_map/all_gather | solution.py:148
  185.6 78.8 %all-gather.8.cloned.1.call-start = ((), (), s32[]{:S(2)}) async-start(), calls=%async_computation.9 | async-start | bytes 2064384 | tf_op jit(solution)/shard_map/all_gather | solution.py:158
  223.2 1.2 copy-start
  247.0 30.5 %copy-start.3 = (f32[256,512]{1,0:T(8,128)S(1)}, f32[256,512]{1,0:T(8,128)}, u32[]{:S(2)}) copy-start(f32[256,512]{1,0:T(8,128)} %fusion.19) | copy-start | bytes 1572868
  270.9 14.5 %all-to-all-start.7 = ((f32[8,1,512]{2,1,0:T(1,128)}), f32[8,1,512]{2,1,0:T(1,128)S(1)}, u32[]{:S(2)}, u32[]{:S(2)}) async-start(f32[8,1,512]{2,1,0:T(1,128)} %broadcast_in_dim.28), calls=%async_computation.7 | async-start | bytes 32768 | tf_op jit(solution)/shard_map/all_to_all | solution.py:116
  280.7 6.5 %copy-start.4 = (bf16[1,256,1792]{2,1,0:T(8,128)(2,1)S(1)}, bf16[1,256,1792]{2,1,0:T(8,128)(2,1)}, u32[]{:S(2)}) copy-start(bf16[1,256,1792]{2,1,0:T(8,128)(2,1)} %param.4) | copy-start | bytes 2752516
Sparse Core Ops, SparseCore 0:
  23.9 45.8 all-gather.9
  185.7 33.2 all-gather.5
  223.3 41.0 all-gather.7

commit v2 on v1

--- a/solution.py
+++ b/solution.py
@@ -112,57 +112,76 @@
     )(gram)
 
 
-def swap_sum(x, axis, dim):
-    return jnp.sum(lax.all_to_all(x, axis, dim, dim, tiled=True), axis=dim)
-
-
-def spread_sum(x, axis, size):
-    return swap_sum(jnp.broadcast_to(x[None], (size,) + x.shape), axis, 0)
+def swap(x, axis):
+    return lax.all_to_all(x, axis, 0, 0, tiled=True)
+
+
+def spread(x, axis):
+    size = lax.axis_size(axis)
+    return swap(jnp.broadcast_to(x[None], (size,) + x.shape), axis)
+
+
+def three_parts(x):
+    high = lax.reduce_precision(x, 8, 7)
+    rest = x - high
+    middle = lax.reduce_precision(rest, 8, 7)
+    return high.astype(bf16), middle.astype(bf16), (rest - middle).astype(bf16)
+
+
+def natural(x):
+    return x.reshape(4, 8, 56, RANK).transpose(1, 0, 2, 3).reshape(8 * 4 * 56, RANK)
 
 
 def on_device(weight, gradient, momentum, basis_in):
     weight_local = weight[0]
     grads = gradient[0].astype(f32)
     basis_low = basis_in[0].astype(bf16)
-    basis_x = lax.all_gather(basis_low, "x", axis=0, tiled=True)
-    basis_all = lax.all_gather(basis_x, "z", axis=0, tiled=True)
-
+
+    basis_z = spread(basis_low, "z").reshape(448, RANK)
+    basis_all = natural(lax.all_gather(basis_z, "x", axis=0, tiled=True))
     squares = jnp.full((1, 128), jnp.sum(grads * grads), f32)
-    squares = spread_sum(squares, ("z", "x"), 32)
-    squares = spread_sum(squares, "y", 8)
-    square_total = lax.psum(squares[0, 0], "core")
+    squares, _ = lax.optimization_barrier((squares, basis_z))
+    squares = jnp.sum(spread(squares, ("z", "x")), axis=0)
+    squares = jnp.sum(spread(squares, "y"), axis=0)
+    square_total = lax.psum(squares, "core")[0, 0]
+
     root_mean = jnp.sqrt(square_total / (2.0 * ROWS * COLS))
     clip_scale = 1.0 / jnp.maximum(1.0, root_mean)
     blend32 = momentum[0].astype(f32) + clip_scale * grads
     blended = blend32.astype(bf16)
 
     partial_left = jnp.dot(blended, basis_all, preferred_element_type=f32)
-    left_rows = swap_sum(partial_left.reshape(8, 32, RANK), "y", 0)
-    left = lax.all_gather(left_rows, "y", axis=0, tiled=True)
+    left_rows = jnp.sum(swap(partial_left.reshape(8, 32, RANK), "y"), axis=0)
+    left = spread(left_rows, "y").reshape(256, RANK)
 
     gram_part = lax.dot_general(left, left, TN, precision=HIGHEST)
-    gram_part = lax.dynamic_slice_in_dim(gram_part, lax.axis_index("y") * 64, 64, axis=0)
-    gram_rows = swap_sum(gram_part.reshape(4, 16, RANK), "x", 0)
-    gram_rows = spread_sum(gram_rows, "z", 8)
-    gram_rows = lax.all_gather(gram_rows, "x", axis=0, tiled=True)
-    gram_matrix = lax.all_gather(gram_rows, "y", axis=0, tiled=True)
-
-    high = lax.reduce_precision(left, 8, 7)
-    low = (left - high).astype(bf16)
-    high = high.astype(bf16)
+    gram_part = lax.dynamic_slice_in_dim(
+        gram_part.reshape(4, 8, 16, RANK), lax.axis_index("y"), 1, axis=1
+    ).reshape(4, 16, RANK)
+    high, low = three_parts(left)[:2]
     product = lax.dot_general(blended, high, TN, preferred_element_type=f32)
     product = product + lax.dot_general(blended, low, TN, preferred_element_type=f32)
-    product = swap_sum(product.reshape(8, 4, 56, RANK), "x", 1)
-    product = swap_sum(product, "z", 0)
-    product_all = lax.all_gather(product.astype(bf16), "x", axis=0, tiled=True)
-    product_all = lax.all_gather(product_all, "z", axis=0, tiled=True)
-
+    product = product.astype(bf16).reshape(8, 4, 56, RANK).transpose(1, 0, 2, 3)
+
+    gram_rows = jnp.sum(swap(gram_part, "x"), axis=0)
+    product = jnp.sum(swap(product.reshape(4, 448, RANK), "x").astype(f32), axis=0)
+    product = jnp.sum(swap(product.reshape(8, 56, RANK), "z"), axis=0)
+    product_low = product.astype(bf16)
+    product_all = lax.all_gather(product_low, ("z", "x"), axis=0, tiled=True)
+    gram_rows, _ = lax.optimization_barrier((gram_rows, product_low))
+    gram_rows = jnp.sum(spread(gram_rows, "z"), axis=0)
+    gram_rows = spread(gram_rows, "y").reshape(128, RANK)
+    gram_matrix = spread(gram_rows, "x").reshape(RANK, RANK)
     inverse_factor = chol_inverse(gram_matrix)
+
     ortho = lax.dot_general(left, inverse_factor, NT, precision=HIGHEST)
     right_own = lax.dot_general(product, inverse_factor, NT, precision=HIGHEST)
-    right_all = lax.dot_general(product_all.astype(f32), inverse_factor, NT, precision=HIGHEST)
-
-    column_squares = spread_sum(jnp.sum(right_all * right_all, axis=0, keepdims=True), "y", 8)
+    high, low = three_parts(inverse_factor)[:2]
+    right_all = lax.dot_general(product_all, high, NT, preferred_element_type=f32)
+    right_all = right_all + lax.dot_general(product_all, low, NT, preferred_element_type=f32)
+
+    column_squares = jnp.sum(right_all * right_all, axis=0, keepdims=True)
+    column_squares = jnp.sum(spread(column_squares, "y"), axis=0)
     right_low = right_all.astype(bf16)
     feedback = lax.dot_general(ortho.astype(bf16), right_low, NT, preferred_element_type=f32)
     new_momentum = (blend32 - (1.0 - momentum_keep) * feedback).astype(bf16)

time: 298 us -> 270 us (0.906)
  blocking collectives: 145 us -> 200 us
  waiting for transfers between devices: 47.8 us -> 4.76 us
  starting transfers between devices: 29.4 us -> 6.62 us
  matrix products: 24.8 us -> 15.4 us
  other arithmetic: 8.65 us -> 3.56 us
    all_to_all x3 -> x11, blocking collectives: 53.6 us -> 198 us  [swap(): return lax.all_to_all(x, axis, 0, 0, tiled=True)]
    all_gather x4 -> x0, blocking collectives: 88 us -> none  [the longest x1 34.1 us: on_device(): gram_rows = lax.all_gather(gram_rows, 'x', axis=0, tiled=True)]
    all_to_all x5 -> x1, starting transfers between devices: 29.3 us -> 6.54 us  [swap(): return lax.all_to_all(x, axis, 0, 0, tiled=True)]
    all_gather x3 -> x2, waiting for transfers between devices: 22.3 us -> 0.02 us  [the longest x1 0.02 us: on_device(): basis_all = natural(lax.all_gather(basis_z, 'x', axis=0, tiled=True))]
    all_to_all x5 -> x1, waiting for transfers between devices: 25.5 us -> 4.7 us  [swap(): return lax.all_to_all(x, axis, 0, 0, tiled=True)]
    reduce_sum x8, other arithmetic: 3.94 us -> 0.47 us  [the longest x1 0.27 us: on_device(): jnp.sum(swap(product.reshape(4, 448, RANK), 'x').astype(f32), axis=0)]
  transfers between devices with their start and end apart: 8 -> 3, of which waited for: 6 -> 1; matrix products, arithmetic and copies ran while one was open for 7% -> 3% of each run, Pallas kernels for 7% -> 8%
where the time goes in v2:
time: 270 us; the launch traced here: 269 us
  blocking collectives  200 us (74%)
  Pallas kernels  20.7 us (8%)
  matrix products  15.4 us (6%)
  between operations  14.4 us (5%)
  starting transfers between devices  6.62 us (2%)
  waiting for transfers between devices  4.76 us (2%)
  local copies, waits for them, and re-layouts  3.6 us (1%)
  other arithmetic  3.56 us (1%)
    all_to_all x11, blocking collectives, swap(): return lax.all_to_all(x, axis, 0, 0, tiled=True)  198 us
    pallas_call x1, Pallas kernels, chol_inverse(): pl.pallas_call(chol_inverse_kernel, out_shape=jax.ShapeDtypeStruct((RANK,...  20.7 us
    all_to_all x1, starting transfers between devices, swap(): return lax.all_to_all(x, axis, 0, 0, tiled=True)  6.54 us
  transfers between devices with their start and end apart: 3, of which 1 were waited for; matrix products, arithmetic and copies ran while one was open for 3% of the time, Pallas kernels for 8%

profile of v2, /device:TPU:6, one launch (start us, length us, event | category | flops | bytes accessed | tf_op | source)
XLA Modules:
  0.0 269.2 jit_solution(7809847810037006597)
XLA Ops:
  7.2 0.0 copy-start.1
  7.2 0.0 copy-start.3
  7.2 0.0 all-gather.3.cloned.1.call-start
  7.2 1.0 convert_bitcast_fusion
  8.3 26.3 %all_to_all.60 = bf16[8,56,512]{2,1,0:T(8,128)(2,1)} all-to-all(bf16[8,56,512]{2,1,0:T(8,128)(2,1)S(1)} %broadcast_in_dim.32), channel_id=1, replica_groups=mesh['z'=8,'x'=4,'y'=8,'core'=2] {'z'}, dimensions={0} | all-to-all | bytes 917504 | tf_op jit(solution)/shard_map/all_to_all | solution.py:116
  34.6 0.0 all-gather.3.cloned.1.call-update
  34.6 0.0 all-gather.5.cloned.1.call-start
  34.7 0.0 copy-done.1
  34.7 1.1 fusion.5
  35.8 0.6 broadcast_in_dim.30
  36.4 12.7 %all_to_all.61 = f32[32,1,128]{2,1,0:T(1,128)S(1)} all-to-all(f32[32,1,128]{2,1,0:T(1,128)S(1)} %broadcast_in_dim.68), channel_id=1, replica_groups=mesh['z'=8,'x'=4,'y'=8,'core'=2] {'z','x'}, dimensions={0} | all-to-all | bytes 32768 | tf_op jit(solution)/shard_map/all_to_all | solution.py:116
  49.2 14.6 %all_to_all.62 = f32[8,1,128]{2,1,0:T(1,128)S(1)} all-to-all(f32[8,1,128]{2,1,0:T(1,128)S(1)} %broadcast_in_dim.69), channel_id=1, replica_groups=mesh['z'=8,'x'=4,'y'=8,'core'=2] {'y'}, dimensions={0} | all-to-all | bytes 8192 | tf_op jit(solution)/shard_map/all_to_all | solution.py:116
  63.8 2.5 psum.7
  66.3 0.0 copy-done.3
  66.4 0.3 fusion.7
  66.6 0.0 all-gather.3.cloned.1.call-done
  66.7 1.7 copy.16
  68.3 0.6 fusion.22
  69.0 20.5 %all_to_all.63 = f32[8,32,512]{2,1,0:T(8,128)S(1)} all-to-all(f32[8,32,512]{2,1,0:T(8,128)S(1)} %fusion.22), channel_id=1, replica_groups=mesh['z'=8,'x'=4,'y'=8,'core'=2] {'y'}, dimensions={0} | all-to-all | bytes 1048576 | tf_op jit(solution)/shard_map/all_to_all | solution.py:116
  89.5 0.1 broadcast_in_dim.70
  89.6 18.5 %all_to_all.64 = f32[8,32,512]{2,1,0:T(8,128)S(1)} all-to-all(f32[8,32,512]{2,1,0:T(8,128)S(1)} %broadcast_in_dim.70), channel_id=1, replica_groups=mesh['z'=8,'x'=4,'y'=8,'core'=2] {'y'}, dimensions={0} | all-to-all | bytes 1048576 | tf_op jit(solution)/shard_map/all_to_all | solution.py:116
  108.1 0.1 fusion.17
  108.1 0.7 fusion.12
  108.8 0.7 add_convert_fusion
  109.5 0.2 copy.18
  109.7 23.2 %all_to_all.65 = bf16[4,448,512]{2,1,0:T(8,128)(2,1)S(1)} all-to-all(bf16[4,448,512]{2,1,0:T(8,128)(2,1)S(1)} %bitcast.71), channel_id=1, replica_groups=mesh['z'=8,'x'=4,'y'=8,'core'=2] {'x'}, dimensions={0} | all-to-all | bytes 3670016 | tf_op jit(solution)/shard_map/all_to_all | solution.py:116
  132.9 0.3 convert_reduce_fusion
  133.2 28.3 %all_to_all.66 = f32[8,56,512]{2,1,0:T(8,128)S(1)} all-to-all(f32[8,56,512]{2,1,0:T(8,128)S(1)} %bitcast.73), channel_id=1, replica_groups=mesh['z'=8,'x'=4,'y'=8,'core'=2] {'z'}, dimensions={0} | all-to-all | bytes 1835008 | tf_op jit(solution)/shard_map/all_to_all | solution.py:116
  161.5 0.1 reduce_sum.99
  161.6 0.6 convert_element_type.93
  162.2 0.0 all-gather.5.cloned.1.call-update
  162.2 0.2 copy.17
  162.4 1.0 fusion.23
  163.5 8.4 %all_to_all.67 = f32[4,16,512]{2,1,0:T(8,128)S(1)} all-to-all(f32[4,16,512]{2,1,0:T(8,128)S(1)} %dynamic-slice_bitcast_fusion), channel_id=1, replica_groups=mesh['z'=8,'x'=4,'y'=8,'core'=2] {'x'}, dimensions={0} | all-to-all | bytes 262144 | tf_op jit(solution)/shard_map/all_to_all | solution.py:116
  171.9 13.2 %all_to_all.68 = f32[8,16,512]{2,1,0:T(8,128)S(1)} all-to-all(f32[8,16,512]{2,1,0:T(8,128)S(1)} %broadcast_in_dim.71), channel_id=1, replica_groups=mesh['z'=8,'x'=4,'y'=8,'core'=2] {'z'}, dimensions={0} | all-to-all | bytes 524288 | tf_op jit(solution)/shard_map/all_to_all | solution.py:116
  185.1 16.0 %all_to_all.69 = f32[8,16,512]{2,1,0:T(8,128)S(1)} all-to-all(f32[8,16,512]{2,1,0:T(8,128)S(1)} %broadcast_in_dim.72), channel_id=1, replica_groups=mesh['z'=8,'x'=4,'y'=8,'core'=2] {'y'}, dimensions={0} | all-to-all | bytes 524288 | tf_op jit(solution)/shard_map/all_to_all | solution.py:116
  201.1 0.1 broadcast_in_dim.74
  201.3 16.0 %all_to_all.70 = f32[4,128,512]{2,1,0:T(8,128)S(1)} all-to-all(f32[4,128,512]{2,1,0:T(8,128)S(1)} %broadcast_in_dim.74), channel_id=1, replica_groups=mesh['z'=8,'x'=4,'y'=8,'core'=2] {'x'}, dimensions={0} | all-to-all | bytes 2097152 | tf_op jit(solution)/shard_map/all_to_all | solution.py:116
  217.3 20.7 %chol_inverse.1 = f32[512,512]{1,0:T(8,128)S(1)} custom-call(f32[512,512]{1,0:T(8,128)S(1)} %bitcast.65), custom_call_target="tpu_custom_call" | custom-call | flops 2000000000 | bytes 2097152 | tf_op jit(solution)/shard_map/chol_inverse/pallas_call | solution.py:103
  238.0 1.9 fusion.24
  239.9 0.0 all-gather.5.cloned.1.call-done
  239.9 0.0 copy-start
  239.9 2.8 %fusion.19 = f32[1792,512]{1,0:T(8,128)S(1)} fusion(bf16[1792,512]{1,0:T(8,128)(2,1)} %all-gather.5.cloned.1.call-done, f32[512,512]{1,0:T(8,128)S(1)} %chol_inverse.1), kind=kOutput, calls=%fused_computation.31 | convolution fusion | flops 940048384 | bytes 6553600 | tf_op jit(solution)/shard_map/dot_general | solution.py:180
  242.7 0.0 copy-done
  242.7 0.0 copy-start.2
  242.7 1.3 multiply_reduce_fusion
  244.0 0.6 broadcast_in_dim.75
  244.6 6.5 %all-to-all-start.11 = ((f32[8,1,512]{2,1,0:T(1,128)}), f32[8,1,512]{2,1,0:T(1,128)S(1)}, u32[]{:S(2)}, u32[]{:S(2)}) async-start(f32[8,1,512]{2,1,0:T(1,128)} %broadcast_in_dim.75), calls=%async_computation.11 | async-start | bytes 32768 | tf_op jit(solution)/shard_map/all_to_all | solution.py:116
  251.1 0.0 copy-done.2
  251.1 3.1 %fusion.4 = bf16[1,256,1792]{2,1,0:T(8,128)(2,1)} fusion(bf16[1,256,1792]{2,1,0:T(8,128)(2,1)} %param.5, bf16[1,256,1792]{2,1,0:T(8,128)(2,1)} %param.6, bf16[1792,512]{1,0:T(8,128)(2,1)S(1)} %get-tuple-element.10, f32[]{:T(128)} %bitcast.7, f32[256,512]{1,0:T(8,128)S(1)} %copy-done.2), kind=kOutput, calls=%fused_computation.10 | convolution fusion | flops 473104384 | bytes 5111812 | tf_op jit(solution)/shard_map/dot_general | solution.py:186
  254.2 4.7 %all-to-all-done.11 = f32[8,1,512]{2,1,0:T(1,128)S(1)} async-done(((f32[8,1,512]{2,1,0:T(1,128)}), f32[8,1,512]{2,1,0:T(1,128)S(1)}, u32[]{:S(2)}, u32[]{:S(2)}) %all-to-all-start.11) | async-done | bytes 16416 | tf_op jit(solution)/shard_map/all_to_all | solution.py:116
  258.9 0.0 copy-start.4
  259.0 1.8 fusion.8
  260.7 0.0 copy-done.4
  260.7 1.6 fusion.3
  (13 shorter events, 0.2 us)
Async XLA Ops:
  7.2 27.5 %copy-start.1 = (bf16[1,256,1792]{2,1,0:T(8,128)(2,1)S(1)}, bf16[1,256,1792]{2,1,0:T(8,128)(2,1)}, u32[]{:S(2)}) copy-start(bf16[1,256,1792]{2,1,0:T(8,128)(2,1)} %param.5) | copy-start | bytes 2752516
  7.2 59.2 %copy-start.3 = (bf16[1,256,1792]{2,1,0:T(8,128)(2,1)S(1)}, bf16[1,256,1792]{2,1,0:T(8,128)(2,1)}, u32[]{:S(2)}) copy-start(bf16[1,256,1792]{2,1,0:T(8,128)(2,1)} %param.6) | copy-start | bytes 2752516
  7.2 59.5 %all-gather.3.cloned.1.call-start = ((), (), s32[]{:S(2)}) async-start(), calls=%async_computation.12 | async-start | bytes 2293760 | tf_op jit(solution)/shard_map/all_gather | solution.py:141
  34.6 205.2 %all-gather.5.cloned.1.call-start = ((), (), s32[]{:S(2)}) async-start(), calls=%async_computation.13 | async-start | bytes 1892352 | tf_op jit(solution)/shard_map/all_gather | solution.py:170
  239.9 2.8 %copy-start = (bf16[1792,512]{1,0:T(8,128)(2,1)S(1)}, bf16[1792,512]{1,0:T(8,128)(2,1)}, u32[]{:S(2)}) copy-start(bf16[1792,512]{1,0:T(8,128)(2,1)} %all-gather.5.cloned.1.call-done) | copy-start | bytes 5505028
  242.7 8.4 %copy-start.2 = (f32[256,512]{1,0:T(8,128)S(1)}, f32[256,512]{1,0:T(8,128)}, u32[]{:S(2)}) copy-start(f32[256,512]{1,0:T(8,128)} %fusion.24) | copy-start | bytes 1572868
  244.6 14.3 %all-to-all-start.11 = ((f32[8,1,512]{2,1,0:T(1,128)}), f32[8,1,512]{2,1,0:T(1,128)S(1)}, u32[]{:S(2)}, u32[]{:S(2)}) async-start(f32[8,1,512]{2,1,0:T(1,128)} %broadcast_in_dim.75), calls=%async_computation.11 | async-start | bytes 32768 | tf_op jit(solution)/shard_map/all_to_all | solution.py:116
  258.9 1.8 copy-start.4
Sparse Core Ops, SparseCore 0:
  34.8 28.4 all-gather.2
  162.3 77.2 all-gather.4

commit v3 on v2

--- a/solution.py
+++ b/solution.py
@@ -128,6 +128,10 @@
     return high.astype(bf16), middle.astype(bf16), (rest - middle).astype(bf16)
 
 
+def from_parts(x):
+    return x[:, :16].astype(f32) + (x[:, 16:32].astype(f32) + x[:, 32:].astype(f32))
+
+
 def natural(x):
     return x.reshape(4, 8, 56, RANK).transpose(1, 0, 2, 3).reshape(8 * 4 * 56, RANK)
 
@@ -163,13 +167,17 @@
     product = product + lax.dot_general(blended, low, TN, preferred_element_type=f32)
     product = product.astype(bf16).reshape(8, 4, 56, RANK).transpose(1, 0, 2, 3)
 
-    gram_rows = jnp.sum(swap(gram_part, "x"), axis=0)
-    product = jnp.sum(swap(product.reshape(4, 448, RANK), "x").astype(f32), axis=0)
-    product = jnp.sum(swap(product.reshape(8, 56, RANK), "z"), axis=0)
-    product_low = product.astype(bf16)
-    product_all = lax.all_gather(product_low, ("z", "x"), axis=0, tiled=True)
-    gram_rows, _ = lax.optimization_barrier((gram_rows, product_low))
-    gram_rows = jnp.sum(spread(gram_rows, "z"), axis=0)
+    both = jnp.concatenate((product.reshape(4, 448, RANK),) + three_parts(gram_part), axis=1)
+    both = swap(both, "x")
+    product = jnp.sum(both[:, :448].astype(f32), axis=0).astype(bf16).reshape(8, 56, RANK)
+    gram_rows = jnp.concatenate(three_parts(jnp.sum(from_parts(both[:, 448:]), axis=0)), axis=0)
+    both = jnp.concatenate((product, jnp.broadcast_to(gram_rows[None], (8, 48, RANK))), axis=1)
+    both = swap(both, "z")
+    product = jnp.sum(both[:, :56].astype(f32), axis=0)
+    gram_rows = jnp.sum(from_parts(both[:, 56:]), axis=0)
+    product_all = spread(product.astype(bf16), "x").reshape(224, RANK)
+    gram_rows, product_all = lax.optimization_barrier((gram_rows, product_all))
+    product_all = lax.all_gather(product_all, "z", axis=0, tiled=True)
     gram_rows = spread(gram_rows, "y").reshape(128, RANK)
     gram_matrix = spread(gram_rows, "x").reshape(RANK, RANK)
     inverse_factor = chol_inverse(gram_matrix)

time: 270 us -> 256 us (0.948)
  blocking collectives: 200 us -> 158 us
  waiting for transfers between devices: 4.76 us -> 24.7 us
  starting transfers between devices: 6.62 us -> 12.3 us
    all_to_all x11 -> x8, blocking collectives: 198 us -> 156 us  [swap(): return lax.all_to_all(x, axis, 0, 0, tiled=True)]
    all_to_all x1 -> x3, waiting for transfers between devices: 4.7 us -> 24.7 us  [swap(): return lax.all_to_all(x, axis, 0, 0, tiled=True)]
    all_to_all x1 -> x3, starting transfers between devices: 6.54 us -> 12.3 us  [swap(): return lax.all_to_all(x, axis, 0, 0, tiled=True)]
  transfers between devices with their start and end apart: 3 -> 5, of which waited for: 1 -> 3; matrix products, arithmetic and copies ran while one was open for 3% -> 3% of each run, Pallas kernels for 8% -> 8%
where the time goes in v3:
time: 256 us; the launch traced here: 255 us
  blocking collectives  158 us (62%)
  waiting for transfers between devices  24.7 us (10%)
  Pallas kernels  20.7 us (8%)
  matrix products  15.4 us (6%)
  between operations  14.5 us (6%)
  starting transfers between devices  12.3 us (5%)
  local copies, waits for them, and re-layouts  5.78 us (2%)
  other arithmetic  3.29 us (1%)
    all_to_all x8, blocking collectives, swap(): return lax.all_to_all(x, axis, 0, 0, tiled=True)  156 us
    all_to_all x3, waiting for transfers between devices, swap(): return lax.all_to_all(x, axis, 0, 0, tiled=True)  24.7 us
    pallas_call x1, Pallas kernels, chol_inverse(): pl.pallas_call(chol_inverse_kernel, out_shape=jax.ShapeDtypeStruct((RANK,...  20.7 us
    all_to_all x3, starting transfers between devices, swap(): return lax.all_to_all(x, axis, 0, 0, tiled=True)  12.3 us
  transfers between devices with their start and end apart: 5, of which 3 were waited for; matrix products, arithmetic and copies ran while one was open for 3% of the time, Pallas kernels for 8%

profile of v3, /device:TPU:6, one launch (start us, length us, event | category | flops | bytes accessed | tf_op | source)
XLA Modules:
  0.0 255.0 jit_solution(11459076032011718315)
XLA Ops:
  7.2 0.0 copy-start.1
  7.2 0.0 copy-start.3
  7.2 0.0 all-gather.3.cloned.1.call-start
  7.2 1.0 convert_bitcast_fusion
  8.3 26.3 %all_to_all.55 = bf16[8,56,512]{2,1,0:T(8,128)(2,1)} all-to-all(bf16[8,56,512]{2,1,0:T(8,128)(2,1)S(1)} %broadcast_in_dim.34), channel_id=1, replica_groups=mesh['z'=8,'x'=4,'y'=8,'core'=2] {'z'}, dimensions={0} | all-to-all | bytes 917504 | tf_op jit(solution)/shard_map/all_to_all | solution.py:116
  34.6 0.0 all-gather.3.cloned.1.call-update
  34.6 0.0 copy-done.1
  34.7 1.1 fusion.5
  35.7 0.6 broadcast_in_dim.32
  36.4 12.7 %all_to_all.56 = f32[32,1,128]{2,1,0:T(1,128)S(1)} all-to-all(f32[32,1,128]{2,1,0:T(1,128)S(1)} %broadcast_in_dim.36), channel_id=1, replica_groups=mesh['z'=8,'x'=4,'y'=8,'core'=2] {'z','x'}, dimensions={0} | all-to-all | bytes 32768 | tf_op jit(solution)/shard_map/all_to_all | solution.py:116
  49.1 14.6 %all_to_all.57 = f32[8,1,128]{2,1,0:T(1,128)S(1)} all-to-all(f32[8,1,128]{2,1,0:T(1,128)S(1)} %broadcast_in_dim.37), channel_id=1, replica_groups=mesh['z'=8,'x'=4,'y'=8,'core'=2] {'y'}, dimensions={0} | all-to-all | bytes 8192 | tf_op jit(solution)/shard_map/all_to_all | solution.py:116
  63.7 2.5 psum.7
  66.3 0.0 copy-done.3
  66.3 0.3 fusion.7
  66.6 0.0 all-gather.3.cloned.1.call-done
  66.6 1.7 copy.16
  68.3 0.6 fusion.24
  68.9 20.5 %all_to_all.58 = f32[8,32,512]{2,1,0:T(8,128)S(1)} all-to-all(f32[8,32,512]{2,1,0:T(8,128)S(1)} %fusion.24), channel_id=1, replica_groups=mesh['z'=8,'x'=4,'y'=8,'core'=2] {'y'}, dimensions={0} | all-to-all | bytes 1048576 | tf_op jit(solution)/shard_map/all_to_all | solution.py:116
  89.5 0.9 broadcast_in_dim.76
  90.4 3.5 %all-to-all-start.4 = ((f32[8,32,512]{2,1,0:T(8,128)}), f32[8,32,512]{2,1,0:T(8,128)S(1)}, u32[]{:S(2)}, u32[]{:S(2)}) async-start(f32[8,32,512]{2,1,0:T(8,128)} %broadcast_in_dim.76), calls=%async_computation.4 | async-start | bytes 1048576 | tf_op jit(solution)/shard_map/all_to_all | solution.py:116
  93.9 15.7 %all-to-all-done.4 = f32[8,32,512]{2,1,0:T(8,128)S(1)} async-done(((f32[8,32,512]{2,1,0:T(8,128)}), f32[8,32,512]{2,1,0:T(8,128)S(1)}, u32[]{:S(2)}, u32[]{:S(2)}) %all-to-all-start.4) | async-done | bytes 524320 | tf_op jit(solution)/shard_map/all_to_all | solution.py:116
  109.5 0.2 copy.18
  109.7 0.1 fusion.17
  109.8 0.7 fusion.12
  110.5 0.7 add_convert_fusion
  111.2 0.2 copy.17
  111.4 1.0 fusion.25
  112.5 0.2 pad_maximum_fusion
  112.6 26.2 %all_to_all.59 = bf16[4,496,512]{2,1,0:T(8,128)(2,1)S(1)} all-to-all(bf16[4,496,512]{2,1,0:T(8,128)(2,1)S(1)} %pad_maximum_fusion), channel_id=1, replica_groups=mesh['z'=8,'x'=4,'y'=8,'core'=2] {'x'}, dimensions={0} | all-to-all | bytes 4063232 | tf_op jit(solution)/shard_map/all_to_all | solution.py:116
  138.9 0.3 slice_reduce_fusion
  139.3 0.1 pad_maximum_fusion.1
  139.3 27.4 %all_to_all.60 = bf16[8,104,512]{2,1,0:T(8,128)(2,1)S(1)} all-to-all(bf16[8,104,512]{2,1,0:T(8,128)(2,1)S(1)} %pad_maximum_fusion.1), channel_id=1, replica_groups=mesh['z'=8,'x'=4,'y'=8,'core'=2] {'z'}, dimensions={0} | all-to-all | bytes 1703936 | tf_op jit(solution)/shard_map/all_to_all | solution.py:116
  166.7 0.1 convert_reduce_fusion
  166.8 0.7 broadcast_in_dim.78
  167.5 5.4 %all-to-all-start.7 = ((bf16[4,56,512]{2,1,0:T(8,128)(2,1)}), bf16[4,56,512]{2,1,0:T(8,128)(2,1)S(1)}, u32[]{:S(2)}, u32[]{:S(2)}) async-start(bf16[4,56,512]{2,1,0:T(8,128)(2,1)} %broadcast_in_dim.78), calls=%async_computation.7 | async-start | bytes 458752 | tf_op jit(solution)/shard_map/all_to_all | solution.py:116
  172.9 0.0 all-gather.5.cloned.1.call-start
  172.9 0.1 add_reduce_fusion
  173.0 4.4 %all-to-all-done.7 = bf16[4,56,512]{2,1,0:T(8,128)(2,1)S(1)} async-done(((bf16[4,56,512]{2,1,0:T(8,128)(2,1)}), bf16[4,56,512]{2,1,0:T(8,128)(2,1)S(1)}, u32[]{:S(2)}, u32[]{:S(2)}) %all-to-all-start.7) | async-done | bytes 229408 | tf_op jit(solution)/shard_map/all_to_all | solution.py:116
  177.3 0.0 copy-start.4
  177.3 0.7 copy-done.4
  178.0 0.0 all-gather.5.cloned.1.call-update
  178.1 14.9 %all_to_all.61 = f32[8,16,512]{2,1,0:T(8,128)S(1)} all-to-all(f32[8,16,512]{2,1,0:T(8,128)S(1)} %broadcast_in_dim.79), channel_id=1, replica_groups=mesh['z'=8,'x'=4,'y'=8,'core'=2] {'y'}, dimensions={0} | all-to-all | bytes 524288 | tf_op jit(solution)/shard_map/all_to_all | solution.py:116
  193.0 0.1 broadcast_in_dim.81
  193.1 13.3 %all_to_all.62 = f32[4,128,512]{2,1,0:T(8,128)S(1)} all-to-all(f32[4,128,512]{2,1,0:T(8,128)S(1)} %broadcast_in_dim.81), channel_id=1, replica_groups=mesh['z'=8,'x'=4,'y'=8,'core'=2] {'x'}, dimensions={0} | all-to-all | bytes 2097152 | tf_op jit(solution)/shard_map/all_to_all | solution.py:116
  206.4 20.7 %chol_inverse.1 = f32[512,512]{1,0:T(8,128)S(1)} custom-call(f32[512,512]{1,0:T(8,128)S(1)} %bitcast.71), custom_call_target="tpu_custom_call" | custom-call | flops 2000000000 | bytes 2097152 | tf_op jit(solution)/shard_map/chol_inverse/pallas_call | solution.py:103
  227.1 1.9 fusion.26
  229.0 0.0 all-gather.5.cloned.1.call-done
  229.0 0.0 copy-start
  229.0 2.8 %fusion.19 = f32[1792,512]{1,0:T(8,128)S(1)} fusion(bf16[1792,512]{1,0:T(8,128)(2,1)} %all-gather.5.cloned.1.call-done, f32[512,512]{1,0:T(8,128)S(1)} %chol_inverse.1), kind=kOutput, calls=%fused_computation.34 | convolution fusion | flops 940048384 | bytes 6553600 | tf_op jit(solution)/shard_map/dot_general | solution.py:188
  231.8 0.0 copy-done
  231.8 0.0 copy-start.2
  231.9 1.3 multiply_reduce_fusion
  233.1 0.6 broadcast_in_dim.82
  233.7 3.3 %all-to-all-start.10 = ((f32[8,1,512]{2,1,0:T(1,128)}), f32[8,1,512]{2,1,0:T(1,128)S(1)}, u32[]{:S(2)}, u32[]{:S(2)}) async-start(f32[8,1,512]{2,1,0:T(1,128)} %broadcast_in_dim.82), calls=%async_computation.10 | async-start | bytes 32768 | tf_op jit(solution)/shard_map/all_to_all | solution.py:116
  237.1 0.0 copy-done.2
  237.1 3.1 %fusion.4 = bf16[1,256,1792]{2,1,0:T(8,128)(2,1)} fusion(bf16[1,256,1792]{2,1,0:T(8,128)(2,1)} %param.5, bf16[1,256,1792]{2,1,0:T(8,128)(2,1)} %param.6, bf16[1792,512]{1,0:T(8,128)(2,1)S(1)} %get-tuple-element.18, f32[]{:T(128)} %bitcast.7, f32[256,512]{1,0:T(8,128)S(1)} %copy-done.2), kind=kOutput, calls=%fused_computation.9 | convolution fusion | flops 473104384 | bytes 5111812 | tf_op jit(solution)/shard_map/dot_general | solution.py:194
  240.2 4.6 %all-to-all-done.10 = f32[8,1,512]{2,1,0:T(1,128)S(1)} async-done(((f32[8,1,512]{2,1,0:T(1,128)}), f32[8,1,512]{2,1,0:T(1,128)S(1)}, u32[]{:S(2)}, u32[]{:S(2)}) %all-to-all-start.10) | async-done | bytes 16416 | tf_op jit(solution)/shard_map/all_to_all | solution.py:116
  244.8 0.0 copy-start.5
  244.8 1.7 fusion.8
  246.6 0.0 copy-done.5
  246.6 1.6 fusion.3
  (15 shorter events, 0.3 us)
Async XLA Ops:
  7.2 27.5 %copy-start.1 = (bf16[1,256,1792]{2,1,0:T(8,128)(2,1)S(1)}, bf16[1,256,1792]{2,1,0:T(8,128)(2,1)}, u32[]{:S(2)}) copy-start(bf16[1,256,1792]{2,1,0:T(8,128)(2,1)} %param.5) | copy-start | bytes 2752516
  7.2 59.1 %copy-start.3 = (bf16[1,256,1792]{2,1,0:T(8,128)(2,1)S(1)}, bf16[1,256,1792]{2,1,0:T(8,128)(2,1)}, u32[]{:S(2)}) copy-start(bf16[1,256,1792]{2,1,0:T(8,128)(2,1)} %param.6) | copy-start | bytes 2752516
  7.2 59.4 %all-gather.3.cloned.1.call-start = ((), (), s32[]{:S(2)}) async-start(), calls=%async_computation.11 | async-start | bytes 2293760 | tf_op jit(solution)/shard_map/all_gather | solution.py:145
  90.4 19.2 %all-to-all-start.4 = ((f32[8,32,512]{2,1,0:T(8,128)}), f32[8,32,512]{2,1,0:T(8,128)S(1)}, u32[]{:S(2)}, u32[]{:S(2)}) async-start(f32[8,32,512]{2,1,0:T(8,128)} %broadcast_in_dim.76), calls=%async_computation.4 | async-start | bytes 1048576 | tf_op jit(solution)/shard_map/all_to_all | solution.py:116
  167.5 9.9 %all-to-all-start.7 = ((bf16[4,56,512]{2,1,0:T(8,128)(2,1)}), bf16[4,56,512]{2,1,0:T(8,128)(2,1)S(1)}, u32[]{:S(2)}, u32[]{:S(2)}) async-start(bf16[4,56,512]{2,1,0:T(8,128)(2,1)} %broadcast_in_dim.78), calls=%async_computation.7 | async-start | bytes 458752 | tf_op jit(solution)/shard_map/all_to_all | solution.py:116
  172.9 56.1 %all-gather.5.cloned.1.call-start = ((), (), s32[]{:S(2)}) async-start(), calls=%async_computation.12 | async-start | bytes 2064384 | tf_op jit(solution)/shard_map/all_gather | solution.py:180
  177.3 0.7 copy-start.4
  229.0 2.8 %copy-start = (bf16[1792,512]{1,0:T(8,128)(2,1)S(1)}, bf16[1792,512]{1,0:T(8,128)(2,1)}, u32[]{:S(2)}) copy-start(bf16[1792,512]{1,0:T(8,128)(2,1)} %all-gather.5.cloned.1.call-done) | copy-start | bytes 5505028
  231.8 5.2 %copy-start.2 = (f32[256,512]{1,0:T(8,128)S(1)}, f32[256,512]{1,0:T(8,128)}, u32[]{:S(2)}) copy-start(f32[256,512]{1,0:T(8,128)} %fusion.26) | copy-start | bytes 1572868
  233.7 11.0 %all-to-all-start.10 = ((f32[8,1,512]{2,1,0:T(1,128)}), f32[8,1,512]{2,1,0:T(1,128)S(1)}, u32[]{:S(2)}, u32[]{:S(2)}) async-start(f32[8,1,512]{2,1,0:T(1,128)} %broadcast_in_dim.82), calls=%async_computation.10 | async-start | bytes 32768 | tf_op jit(solution)/shard_map/all_to_all | solution.py:116
  244.8 1.8 copy-start.5
Sparse Core Ops, SparseCore 0:
  34.8 28.4 all-gather.2
  178.2 37.2 all-gather.4

commit v4 on v3

--- a/solution.py
+++ b/solution.py
@@ -22,6 +22,7 @@
 f32 = jnp.float32
 bf16 = jnp.bfloat16
 HIGHEST = lax.Precision.HIGHEST
+NN = (((1,), (0,)), ((), ()))
 TN = (((0,), (0,)), ((), ()))
 NT = (((1,), (1,)), ((), ()))
 
@@ -79,24 +80,36 @@
     return jnp.concatenate([inverse[v] * scale[v] for v in range(tiles)], axis=0)
 
 
+def exact(a, b, dims):
+    return lax.dot_general(a, b, dims, precision=HIGHEST, preferred_element_type=f32)
+
+
 def chol_inverse_kernel(gram_ref, out_ref, work_ref):
     work_ref[:, :RANK] = gram_ref[...]
     i = lax.broadcasted_iota(jnp.int32, (RANK, RANK), 0)
     j = lax.broadcasted_iota(jnp.int32, (RANK, RANK), 1)
     work_ref[:, RANK:] = jnp.where(i == j, 1.0, 0.0).astype(f32)
+    ahead = gram_ref[:BLOCK, :BLOCK]
     for k in range(0, RANK, BLOCK):
         end = k + BLOCK
-        left = RANK - end
-        inverse = block_inverse(work_ref[k:end, k:end])
-        wide = jnp.dot(
-            inverse, work_ref[k:end, end : RANK + end], precision=HIGHEST, preferred_element_type=f32
+        far = end + BLOCK
+        left = RANK - far
+        inverse = block_inverse(ahead)
+        if end == RANK:
+            out_ref[k:, :] = exact(inverse, work_ref[k:, end:], NN)
+            break
+        near = exact(inverse, work_ref[k:end, end:far], NN)
+        ahead = work_ref[end:far, end:far] - exact(near, near, TN)
+        wide = exact(inverse, work_ref[k:end, far : RANK + end], NN)
+        work_ref[end:far, far : RANK + end] = work_ref[end:far, far : RANK + end] - exact(
+            near, wide, TN
         )
+        if left:
+            work_ref[far:, far : RANK + end] = work_ref[far:, far : RANK + end] - exact(
+                wide[:, :left], wide, TN
+            )
         out_ref[k:end, :end] = wide[:, left:]
-        if left:
-            out_ref[k:end, end:] = jnp.zeros((BLOCK, left), f32)
-            work_ref[end:, end : RANK + end] = work_ref[end:, end : RANK + end] - lax.dot_general(
-                wide[:, :left], wide, TN, precision=HIGHEST, preferred_element_type=f32
-            )
+        out_ref[k:end, end:] = jnp.zeros((BLOCK, RANK - end), f32)
 
 
 def chol_inverse(gram):
@@ -121,15 +134,13 @@
     return swap(jnp.broadcast_to(x[None], (size,) + x.shape), axis)
 
 
-def three_parts(x):
+def two_parts(x):
     high = lax.reduce_precision(x, 8, 7)
-    rest = x - high
-    middle = lax.reduce_precision(rest, 8, 7)
-    return high.astype(bf16), middle.astype(bf16), (rest - middle).astype(bf16)
+    return high.astype(bf16), (x - high).astype(bf16)
 
 
 def from_parts(x):
-    return x[:, :16].astype(f32) + (x[:, 16:32].astype(f32) + x[:, 32:].astype(f32))
+    return x[:, :16].astype(f32) + x[:, 16:].astype(f32)
 
 
 def natural(x):
@@ -162,16 +173,16 @@
     gram_part = lax.dynamic_slice_in_dim(
         gram_part.reshape(4, 8, 16, RANK), lax.axis_index("y"), 1, axis=1
     ).reshape(4, 16, RANK)
-    high, low = three_parts(left)[:2]
+    high, low = two_parts(left)
     product = lax.dot_general(blended, high, TN, preferred_element_type=f32)
     product = product + lax.dot_general(blended, low, TN, preferred_element_type=f32)
     product = product.astype(bf16).reshape(8, 4, 56, RANK).transpose(1, 0, 2, 3)
 
-    both = jnp.concatenate((product.reshape(4, 448, RANK),) + three_parts(gram_part), axis=1)
+    both = jnp.concatenate((product.reshape(4, 448, RANK),) + two_parts(gram_part), axis=1)
     both = swap(both, "x")
     product = jnp.sum(both[:, :448].astype(f32), axis=0).astype(bf16).reshape(8, 56, RANK)
-    gram_rows = jnp.concatenate(three_parts(jnp.sum(from_parts(both[:, 448:]), axis=0)), axis=0)
-    both = jnp.concatenate((product, jnp.broadcast_to(gram_rows[None], (8, 48, RANK))), axis=1)
+    gram_rows = jnp.concatenate(two_parts(jnp.sum(from_parts(both[:, 448:]), axis=0)), axis=0)
+    both = jnp.concatenate((product, jnp.broadcast_to(gram_rows[None], (8, 32, RANK))), axis=1)
     both = swap(both, "z")
     product = jnp.sum(both[:, :56].astype(f32), axis=0)
     gram_rows = jnp.sum(from_parts(both[:, 56:]), axis=0)
@@ -182,13 +193,15 @@
     gram_matrix = spread(gram_rows, "x").reshape(RANK, RANK)
     inverse_factor = chol_inverse(gram_matrix)
 
+    high, low = two_parts(inverse_factor)
+    right_all = lax.dot_general(product_all, high, NT, preferred_element_type=f32)
+    right_all = right_all + lax.dot_general(product_all, low, NT, preferred_element_type=f32)
+    column_squares = jnp.sum(right_all * right_all, axis=0, keepdims=True)
+    column_squares, inverse_factor = lax.optimization_barrier((column_squares, inverse_factor))
+
     ortho = lax.dot_general(left, inverse_factor, NT, precision=HIGHEST)
     right_own = lax.dot_general(product, inverse_factor, NT, precision=HIGHEST)
-    high, low = three_parts(inverse_factor)[:2]
-    right_all = lax.dot_general(product_all, high, NT, preferred_element_type=f32)
-    right_all = right_all + lax.dot_general(product_all, low, NT, preferred_element_type=f32)
-
-    column_squares = jnp.sum(right_all * right_all, axis=0, keepdims=True)
+    ortho, right_own = lax.optimization_barrier((ortho, right_own))
     column_squares = jnp.sum(spread(column_squares, "y"), axis=0)
     right_low = right_all.astype(bf16)
     feedback = lax.dot_general(ortho.astype(bf16), right_low, NT, preferred_element_type=f32)

time: 256 us -> 252 us (0.984)
  blocking collectives: 158 us -> 155 us
    all_to_all x8, blocking collectives: 156 us -> 153 us  [swap(): return lax.all_to_all(x, axis, 0, 0, tiled=True)]
  transfers between devices with their start and end apart: 5 -> 5, of which waited for: 3 -> 3; matrix products, arithmetic and copies ran while one was open for 3% -> 2% of each run, Pallas kernels for 8% -> 8%
where the time goes in v4:
time: 252 us; the launch traced here: 251 us
  blocking collectives  155 us (62%)
  waiting for transfers between devices  24.5 us (10%)
  Pallas kernels  19.1 us (8%)
  matrix products  15.6 us (6%)
  between operations  14.5 us (6%)
  starting transfers between devices  12.3 us (5%)
  local copies, waits for them, and re-layouts  5.75 us (2%)
  other arithmetic  3.85 us (2%)
    all_to_all x8, blocking collectives, swap(): return lax.all_to_all(x, axis, 0, 0, tiled=True)  153 us
    all_to_all x3, waiting for transfers between devices, swap(): return lax.all_to_all(x, axis, 0, 0, tiled=True)  24.4 us
    pallas_call x1, Pallas kernels, chol_inverse(): pl.pallas_call(chol_inverse_kernel, out_shape=jax.ShapeDtypeStruct((RANK,...  19.1 us
    all_to_all x3, starting transfers between devices, swap(): return lax.all_to_all(x, axis, 0, 0, tiled=True)  12.3 us
  transfers between devices with their start and end apart: 5, of which 3 were waited for; matrix products, arithmetic and copies ran while one was open for 2% of the time, Pallas kernels for 8%

profile of v4, /device:TPU:6, one launch (start us, length us, event | category | flops | bytes accessed | tf_op | source)
XLA Modules:
  0.0 250.7 jit_solution(10897394443618017718)
XLA Ops:
  7.2 0.0 copy-start.1
  7.2 0.0 copy-start.3
  7.2 0.0 all-gather.3.cloned.1.call-start
  7.2 1.0 convert_bitcast_fusion
  8.3 26.3 %all_to_all.55 = bf16[8,56,512]{2,1,0:T(8,128)(2,1)} all-to-all(bf16[8,56,512]{2,1,0:T(8,128)(2,1)S(1)} %broadcast_in_dim.38), channel_id=1, replica_groups=mesh['z'=8,'x'=4,'y'=8,'core'=2] {'z'}, dimensions={0} | all-to-all | bytes 917504 | tf_op jit(solution)/shard_map/all_to_all | solution.py:129
  34.6 0.0 all-gather.3.cloned.1.call-update
  34.6 0.0 copy-done.1
  34.7 1.1 fusion.5
  35.7 0.6 broadcast_in_dim.36
  36.4 12.7 %all_to_all.56 = f32[32,1,128]{2,1,0:T(1,128)S(1)} all-to-all(f32[32,1,128]{2,1,0:T(1,128)S(1)} %broadcast_in_dim.80), channel_id=1, replica_groups=mesh['z'=8,'x'=4,'y'=8,'core'=2] {'z','x'}, dimensions={0} | all-to-all | bytes 32768 | tf_op jit(solution)/shard_map/all_to_all | solution.py:129
  49.1 14.6 %all_to_all.57 = f32[8,1,128]{2,1,0:T(1,128)S(1)} all-to-all(f32[8,1,128]{2,1,0:T(1,128)S(1)} %broadcast_in_dim.81), channel_id=1, replica_groups=mesh['z'=8,'x'=4,'y'=8,'core'=2] {'y'}, dimensions={0} | all-to-all | bytes 8192 | tf_op jit(solution)/shard_map/all_to_all | solution.py:129
  63.7 2.5 psum.7
  66.3 0.0 copy-done.3
  66.3 0.3 fusion.7
  66.6 0.0 all-gather.3.cloned.1.call-done
  66.6 1.7 copy.16
  68.3 0.6 fusion.21
  68.9 20.5 %all_to_all.58 = f32[8,32,512]{2,1,0:T(8,128)S(1)} all-to-all(f32[8,32,512]{2,1,0:T(8,128)S(1)} %fusion.21), channel_id=1, replica_groups=mesh['z'=8,'x'=4,'y'=8,'core'=2] {'y'}, dimensions={0} | all-to-all | bytes 1048576 | tf_op jit(solution)/shard_map/all_to_all | solution.py:129
  89.5 0.9 broadcast_in_dim.82
  90.4 3.5 %all-to-all-start.4 = ((f32[8,32,512]{2,1,0:T(8,128)}), f32[8,32,512]{2,1,0:T(8,128)S(1)}, u32[]{:S(2)}, u32[]{:S(2)}) async-start(f32[8,32,512]{2,1,0:T(8,128)} %broadcast_in_dim.82), calls=%async_computation.4 | async-start | bytes 1048576 | tf_op jit(solution)/shard_map/all_to_all | solution.py:129
  93.9 15.7 %all-to-all-done.4 = f32[8,32,512]{2,1,0:T(8,128)S(1)} async-done(((f32[8,32,512]{2,1,0:T(8,128)}), f32[8,32,512]{2,1,0:T(8,128)S(1)}, u32[]{:S(2)}, u32[]{:S(2)}) %all-to-all-start.4) | async-done | bytes 524320 | tf_op jit(solution)/shard_map/all_to_all | solution.py:129
  109.5 0.2 copy.18
  109.7 0.1 fusion.14
  109.8 0.7 fusion.10
  110.5 0.7 add_convert_fusion
  111.2 0.1 copy.17
  111.4 1.0 fusion.22
  112.4 0.1 pad_maximum_fusion
  112.6 25.5 %all_to_all.59 = bf16[4,480,512]{2,1,0:T(8,128)(2,1)S(1)} all-to-all(bf16[4,480,512]{2,1,0:T(8,128)(2,1)S(1)} %pad_maximum_fusion), channel_id=1, replica_groups=mesh['z'=8,'x'=4,'y'=8,'core'=2] {'x'}, dimensions={0} | all-to-all | bytes 3932160 | tf_op jit(solution)/shard_map/all_to_all | solution.py:129
  138.2 0.3 slice_reduce_fusion
  138.5 0.1 pad_maximum_fusion.1
  138.5 24.8 %all_to_all.60 = bf16[8,88,512]{2,1,0:T(8,128)(2,1)S(1)} all-to-all(bf16[8,88,512]{2,1,0:T(8,128)(2,1)S(1)} %pad_maximum_fusion.1), channel_id=1, replica_groups=mesh['z'=8,'x'=4,'y'=8,'core'=2] {'z'}, dimensions={0} | all-to-all | bytes 1441792 | tf_op jit(solution)/shard_map/all_to_all | solution.py:129
  163.3 0.1 convert_reduce_fusion
  163.4 0.7 broadcast_in_dim.84
  164.1 5.4 %all-to-all-start.7 = ((bf16[4,56,512]{2,1,0:T(8,128)(2,1)}), bf16[4,56,512]{2,1,0:T(8,128)(2,1)S(1)}, u32[]{:S(2)}, u32[]{:S(2)}) async-start(bf16[4,56,512]{2,1,0:T(8,128)(2,1)} %broadcast_in_dim.84), calls=%async_computation.7 | async-start | bytes 458752 | tf_op jit(solution)/shard_map/all_to_all | solution.py:129
  169.6 0.0 all-gather.5.cloned.1.call-start
  169.6 4.4 %all-to-all-done.7 = bf16[4,56,512]{2,1,0:T(8,128)(2,1)S(1)} async-done(((bf16[4,56,512]{2,1,0:T(8,128)(2,1)}), bf16[4,56,512]{2,1,0:T(8,128)(2,1)S(1)}, u32[]{:S(2)}, u32[]{:S(2)}) %all-to-all-start.7) | async-done | bytes 229408 | tf_op jit(solution)/shard_map/all_to_all | solution.py:129
  174.0 0.0 copy-start.4
  174.0 0.7 copy-done.4
  174.7 0.0 all-gather.5.cloned.1.call-update
  174.7 14.9 %all_to_all.61 = f32[8,16,512]{2,1,0:T(8,128)S(1)} all-to-all(f32[8,16,512]{2,1,0:T(8,128)S(1)} %broadcast_in_dim.85), channel_id=1, replica_groups=mesh['z'=8,'x'=4,'y'=8,'core'=2] {'y'}, dimensions={0} | all-to-all | bytes 524288 | tf_op jit(solution)/shard_map/all_to_all | solution.py:129
  189.6 0.1 broadcast_in_dim.87
  189.7 13.3 %all_to_all.62 = f32[4,128,512]{2,1,0:T(8,128)S(1)} all-to-all(f32[4,128,512]{2,1,0:T(8,128)S(1)} %broadcast_in_dim.87), channel_id=1, replica_groups=mesh['z'=8,'x'=4,'y'=8,'core'=2] {'x'}, dimensions={0} | all-to-all | bytes 2097152 | tf_op jit(solution)/shard_map/all_to_all | solution.py:129
  203.1 19.1 %chol_inverse.1 = f32[512,512]{1,0:T(8,128)S(1)} custom-call(f32[512,512]{1,0:T(8,128)S(1)} %bitcast.69), custom_call_target="tpu_custom_call" | custom-call | flops 2000000000 | bytes 2097152 | tf_op jit(solution)/shard_map/chol_inverse/pallas_call | solution.py:116
  222.2 0.0 all-gather.5.cloned.1.call-done
  222.2 0.0 copy-start
  222.2 2.8 %fusion.16 = f32[1792,512]{1,0:T(8,128)S(1)} fusion(bf16[1792,512]{1,0:T(8,128)(2,1)} %all-gather.5.cloned.1.call-done, f32[512,512]{1,0:T(8,128)S(1)} %chol_inverse.1), kind=kOutput, calls=%fused_computation.30 | convolution fusion | flops 940048384 | bytes 6553600 | tf_op jit(solution)/shard_map/dot_general | solution.py:197
  225.0 0.0 copy-done
  225.1 1.3 multiply_reduce_fusion
  226.3 1.7 fusion.24
  228.1 1.9 fusion.23
  229.9 0.6 broadcast_in_dim.90
  230.5 3.3 %all-to-all-start.10 = ((f32[8,1,512]{2,1,0:T(1,128)}), f32[8,1,512]{2,1,0:T(1,128)S(1)}, u32[]{:S(2)}, u32[]{:S(2)}) async-start(f32[8,1,512]{2,1,0:T(1,128)} %broadcast_in_dim.90), calls=%async_computation.10 | async-start | bytes 32768 | tf_op jit(solution)/shard_map/all_to_all | solution.py:129
  233.9 0.0 copy-start.6
  233.9 0.0 copy-start.2
  233.9 0.0 copy-start.5
  233.9 3.3 %fusion.4 = bf16[1,256,1792]{2,1,0:T(8,128)(2,1)} fusion(bf16[1,256,1792]{2,1,0:T(8,128)(2,1)} %param.5, bf16[1,256,1792]{2,1,0:T(8,128)(2,1)} %param.6, bf16[1792,512]{1,0:T(8,128)(2,1)S(1)} %get-tuple-element.24, f32[]{:T(128)} %bitcast.7, f32[256,512]{1,0:T(8,128)} %fusion.23), kind=kOutput, calls=%fused_computation.9 | convolution fusion | flops 473104384 | bytes 5111812 | tf_op jit(solution)/shard_map/dot_general | solution.py:207
  237.2 4.3 %all-to-all-done.10 = f32[8,1,512]{2,1,0:T(1,128)S(1)} async-done(((f32[8,1,512]{2,1,0:T(1,128)}), f32[8,1,512]{2,1,0:T(1,128)S(1)}, u32[]{:S(2)}, u32[]{:S(2)}) %all-to-all-start.10) | async-done | bytes 16416 | tf_op jit(solution)/shard_map/all_to_all | solution.py:129
  241.6 0.0 copy-done.6
  241.6 0.7 multiply_bitcast_fusion
  242.3 0.0 copy-done.2
  242.3 0.0 copy-done.5
  242.3 1.6 fusion.3
  (16 shorter events, 0.3 us)
Async XLA Ops:
  7.2 27.5 %copy-start.1 = (bf16[1,256,1792]{2,1,0:T(8,128)(2,1)S(1)}, bf16[1,256,1792]{2,1,0:T(8,128)(2,1)}, u32[]{:S(2)}) copy-start(bf16[1,256,1792]{2,1,0:T(8,128)(2,1)} %param.5) | copy-start | bytes 2752516
  7.2 59.1 %copy-start.3 = (bf16[1,256,1792]{2,1,0:T(8,128)(2,1)S(1)}, bf16[1,256,1792]{2,1,0:T(8,128)(2,1)}, u32[]{:S(2)}) copy-start(bf16[1,256,1792]{2,1,0:T(8,128)(2,1)} %param.6) | copy-start | bytes 2752516
  7.2 59.4 %all-gather.3.cloned.1.call-start = ((), (), s32[]{:S(2)}) async-start(), calls=%async_computation.11 | async-start | bytes 2293760 | tf_op jit(solution)/shard_map/all_gather | solution.py:156
  90.4 19.2 %all-to-all-start.4 = ((f32[8,32,512]{2,1,0:T(8,128)}), f32[8,32,512]{2,1,0:T(8,128)S(1)}, u32[]{:S(2)}, u32[]{:S(2)}) async-start(f32[8,32,512]{2,1,0:T(8,128)} %broadcast_in_dim.82), calls=%async_computation.4 | async-start | bytes 1048576 | tf_op jit(solution)/shard_map/all_to_all | solution.py:129
  164.1 9.9 %all-to-all-start.7 = ((bf16[4,56,512]{2,1,0:T(8,128)(2,1)}), bf16[4,56,512]{2,1,0:T(8,128)(2,1)S(1)}, u32[]{:S(2)}, u32[]{:S(2)}) async-start(bf16[4,56,512]{2,1,0:T(8,128)(2,1)} %broadcast_in_dim.84), calls=%async_computation.7 | async-start | bytes 458752 | tf_op jit(solution)/shard_map/all_to_all | solution.py:129
  169.6 52.6 %all-gather.5.cloned.1.call-start = ((), (), s32[]{:S(2)}) async-start(), calls=%async_computation.12 | async-start | bytes 2064384 | tf_op jit(solution)/shard_map/all_gather | solution.py:191
  174.0 0.7 copy-start.4
  222.2 2.8 %copy-start = (bf16[1792,512]{1,0:T(8,128)(2,1)S(1)}, bf16[1792,512]{1,0:T(8,128)(2,1)}, u32[]{:S(2)}) copy-start(bf16[1792,512]{1,0:T(8,128)(2,1)} %all-gather.5.cloned.1.call-done) | copy-start | bytes 5505028
  230.5 11.0 %all-to-all-start.10 = ((f32[8,1,512]{2,1,0:T(1,128)}), f32[8,1,512]{2,1,0:T(1,128)S(1)}, u32[]{:S(2)}, u32[]{:S(2)}) async-start(f32[8,1,512]{2,1,0:T(1,128)} %broadcast_in_dim.90), calls=%async_computation.10 | async-start | bytes 32768 | tf_op jit(solution)/shard_map/all_to_all | solution.py:129
  233.9 7.7 %copy-start.6 = (f32[56,512]{1,0:T(8,128)S(1)}, f32[56,512]{1,0:T(8,128)}, u32[]{:S(2)}) copy-start(f32[56,512]{1,0:T(8,128)} %fusion.24) | copy-start | bytes 344068
  233.9 8.4 %copy-start.2 = (f32[256,512]{1,0:T(8,128)S(1)}, f32[256,512]{1,0:T(8,128)}, u32[]{:S(2)}) copy-start(f32[256,512]{1,0:T(8,128)} %fusion.23) | copy-start | bytes 1572868
  233.9 8.4 %copy-start.5 = (bf16[1,256,1792]{2,1,0:T(8,128)(2,1)S(1)}, bf16[1,256,1792]{2,1,0:T(8,128)(2,1)}, u32[]{:S(2)}) copy-start(bf16[1,256,1792]{2,1,0:T(8,128)(2,1)} %param.4) | copy-start | bytes 2752516
Sparse Core Ops, SparseCore 0:
  34.8 28.4 all-gather.2
  174.8 37.2 all-gather.4

commit v5 on v4

--- a/solution.py
+++ b/solution.py
@@ -153,12 +153,14 @@
     basis_low = basis_in[0].astype(bf16)
 
     basis_z = spread(basis_low, "z").reshape(448, RANK)
-    basis_all = natural(lax.all_gather(basis_z, "x", axis=0, tiled=True))
     squares = jnp.full((1, 128), jnp.sum(grads * grads), f32)
-    squares, _ = lax.optimization_barrier((squares, basis_z))
-    squares = jnp.sum(spread(squares, ("z", "x")), axis=0)
-    squares = jnp.sum(spread(squares, "y"), axis=0)
-    square_total = lax.psum(squares, "core")[0, 0]
+    squares = lax.psum(lax.psum(squares, "core"), "x")
+    basis_z, squares = lax.optimization_barrier((basis_z, squares))
+    basis_x = spread(basis_z, "x")
+    squares = lax.psum(lax.psum(squares, "y"), "z")
+    basis_x, squares = lax.optimization_barrier((basis_x, squares))
+    basis_all = natural(basis_x)
+    square_total = squares[0, 0]
 
     root_mean = jnp.sqrt(square_total / (2.0 * ROWS * COLS))
     clip_scale = 1.0 / jnp.maximum(1.0, root_mean)

time: 252 us -> 242 us (0.960)
  blocking collectives: 155 us -> 125 us
  starting transfers between devices: 12.3 us -> 27.4 us
    all_to_all x8 -> x5, blocking collectives: 153 us -> 81.9 us  [swap(): return lax.all_to_all(x, axis, 0, 0, tiled=True)]
    psum x1 -> x4, blocking collectives: 2.46 us -> 43.5 us  [the longest x2 33.5 us: on_device(): squares = lax.psum(lax.psum(squares, 'y'), 'z')]
    all_to_all x3 -> x5, starting transfers between devices: 12.3 us -> 27.4 us  [swap(): return lax.all_to_all(x, axis, 0, 0, tiled=True)]
    all_to_all x3 -> x5, waiting for transfers between devices: 24.4 us -> 26.4 us  [swap(): return lax.all_to_all(x, axis, 0, 0, tiled=True)]
  transfers between devices with their start and end apart: 5 -> 6, of which waited for: 3 -> 4; matrix products, arithmetic and copies ran while one was open for 2% -> 2% of each run, Pallas kernels for 8% -> 8%
where the time goes in v5:
time: 242 us; the launch traced here: 240 us
  blocking collectives  125 us (52%)
  starting transfers between devices  27.4 us (11%)
  waiting for transfers between devices  26.4 us (11%)
  Pallas kernels  19.1 us (8%)
  matrix products  15.6 us (6%)
  between operations  14.4 us (6%)
  local copies, waits for them, and re-layouts  7.95 us (3%)
  other arithmetic  3.78 us (2%)
    all_to_all x5, blocking collectives, swap(): return lax.all_to_all(x, axis, 0, 0, tiled=True)  81.9 us
    psum x2, blocking collectives, on_device(): squares = lax.psum(lax.psum(squares, 'y'), 'z')  33.5 us
    all_to_all x5, starting transfers between devices, swap(): return lax.all_to_all(x, axis, 0, 0, tiled=True)  27.4 us
    all_to_all x5, waiting for transfers between devices, swap(): return lax.all_to_all(x, axis, 0, 0, tiled=True)  26.4 us
    pallas_call x1, Pallas kernels, chol_inverse(): pl.pallas_call(chol_inverse_kernel, out_shape=jax.ShapeDtypeStruct((RANK,...  19.1 us
    psum x2, blocking collectives, on_device(): squares = lax.psum(lax.psum(squares, 'core'), 'x')  9.92 us
  transfers between devices with their start and end apart: 6, of which 4 were waited for; matrix products, arithmetic and copies ran while one was open for 2% of the time, Pallas kernels for 8%

profile of v5, /device:TPU:6, one launch (start us, length us, event | category | flops | bytes accessed | tf_op | source)
XLA Modules:
  0.0 240.0 jit_solution(6109672646411361863)
XLA Ops:
  7.2 0.0 copy-start.1
  7.2 1.0 convert_bitcast_fusion
  8.2 0.8 broadcast_in_dim.33
  9.0 10.3 %all-to-all-start = ((bf16[8,56,512]{2,1,0:T(8,128)(2,1)}), bf16[8,56,512]{2,1,0:T(8,128)(2,1)S(1)}, u32[]{:S(2)}, u32[]{:S(2)}) async-start(bf16[8,56,512]{2,1,0:T(8,128)(2,1)} %broadcast_in_dim.33), calls=%async_computation | async-start | bytes 917504 | tf_op jit(solution)/shard_map/all_to_all | solution.py:129
  19.3 0.0 copy-done.1
  19.3 1.1 fusion.5
  20.4 0.6 broadcast_in_dim.34
  21.0 2.5 %psum.28 = f32[1,128]{1,0:T(1,128)S(1)} all-reduce(f32[1,128]{1,0:T(1,128)S(1)} %broadcast_in_dim.34), channel_id=1, replica_groups=mesh['z'=8,'x'=4,'y'=8,'core'=2] {'core'}, use_global_device_ids=true, to_apply=%region_1.0 | all-reduce | flops 128 | bytes 1024 | tf_op jit(solution)/shard_map/psum | solution.py:157
  23.5 7.4 %psum.29 = f32[1,128]{1,0:T(1,128)S(1)} all-reduce(f32[1,128]{1,0:T(1,128)S(1)} %psum.28), channel_id=1, replica_groups=mesh['z'=8,'x'=4,'y'=8,'core'=2] {'x'}, use_global_device_ids=true, to_apply=%region_2.0 | all-reduce | flops 128 | bytes 1024 | tf_op jit(solution)/shard_map/psum | solution.py:157
  30.9 4.4 %all-to-all-done = bf16[8,56,512]{2,1,0:T(8,128)(2,1)S(1)} async-done(((bf16[8,56,512]{2,1,0:T(8,128)(2,1)}), bf16[8,56,512]{2,1,0:T(8,128)(2,1)S(1)}, u32[]{:S(2)}, u32[]{:S(2)}) %all-to-all-start) | async-done | bytes 458784 | tf_op jit(solution)/shard_map/all_to_all | solution.py:129
  35.4 1.4 broadcast_in_dim.35
  36.7 4.8 %all-to-all-start.1 = ((bf16[4,448,512]{2,1,0:T(8,128)(2,1)}), bf16[4,448,512]{2,1,0:T(8,128)(2,1)}, u32[]{:S(2)}, u32[]{:S(2)}) async-start(bf16[4,448,512]{2,1,0:T(8,128)(2,1)} %broadcast_in_dim.35), calls=%async_computation.1 | async-start | bytes 3670016 | tf_op jit(solution)/shard_map/all_to_all | solution.py:129
  41.6 17.6 %psum.30 = f32[1,128]{1,0:T(1,128)S(1)} all-reduce(f32[1,128]{1,0:T(1,128)S(1)} %psum.29), channel_id=1, replica_groups=mesh['z'=8,'x'=4,'y'=8,'core'=2] {'y'}, use_global_device_ids=true, to_apply=%region_3.0 | all-reduce | flops 128 | bytes 1024 | tf_op jit(solution)/shard_map/psum | solution.py:160
  59.2 15.9 %psum.31 = f32[1,128]{1,0:T(1,128)S(1)} all-reduce(f32[1,128]{1,0:T(1,128)S(1)} %psum.30), channel_id=1, replica_groups=mesh['z'=8,'x'=4,'y'=8,'core'=2] {'z'}, use_global_device_ids=true, to_apply=%region_4.0 | all-reduce | flops 128 | bytes 1024 | tf_op jit(solution)/shard_map/psum | solution.py:160
  75.1 0.0 all-to-all-done.1
  75.2 0.0 copy-start.3
  75.3 1.8 copy.16
  77.0 0.0 copy-done.3
  77.0 0.3 fusion.7
  77.3 0.6 fusion.21
  78.0 17.4 %all_to_all.50 = f32[8,32,512]{2,1,0:T(8,128)S(1)} all-to-all(f32[8,32,512]{2,1,0:T(8,128)S(1)} %fusion.21), channel_id=1, replica_groups=mesh['z'=8,'x'=4,'y'=8,'core'=2] {'y'}, dimensions={0} | all-to-all | bytes 1048576 | tf_op jit(solution)/shard_map/all_to_all | solution.py:129
  95.4 0.9 broadcast_in_dim.72
  96.2 3.5 %all-to-all-start.3 = ((f32[8,32,512]{2,1,0:T(8,128)}), f32[8,32,512]{2,1,0:T(8,128)S(1)}, u32[]{:S(2)}, u32[]{:S(2)}) async-start(f32[8,32,512]{2,1,0:T(8,128)} %broadcast_in_dim.72), calls=%async_computation.3 | async-start | bytes 1048576 | tf_op jit(solution)/shard_map/all_to_all | solution.py:129
  99.8 13.2 %all-to-all-done.3 = f32[8,32,512]{2,1,0:T(8,128)S(1)} async-done(((f32[8,32,512]{2,1,0:T(8,128)}), f32[8,32,512]{2,1,0:T(8,128)S(1)}, u32[]{:S(2)}, u32[]{:S(2)}) %all-to-all-start.3) | async-done | bytes 524320 | tf_op jit(solution)/shard_map/all_to_all | solution.py:129
  113.0 0.2 copy.18
  113.2 0.1 fusion.14
  113.2 0.7 fusion.10
  113.9 0.7 add_convert_fusion
  114.6 0.1 copy.17
  114.8 1.0 fusion.22
  115.8 0.1 pad_maximum_fusion
  116.0 18.5 %all_to_all.51 = bf16[4,480,512]{2,1,0:T(8,128)(2,1)S(1)} all-to-all(bf16[4,480,512]{2,1,0:T(8,128)(2,1)S(1)} %pad_maximum_fusion), channel_id=1, replica_groups=mesh['z'=8,'x'=4,'y'=8,'core'=2] {'x'}, dimensions={0} | all-to-all | bytes 3932160 | tf_op jit(solution)/shard_map/all_to_all | solution.py:129
  134.6 0.3 slice_reduce_fusion
  134.9 0.1 pad_maximum_fusion.1
  134.9 19.8 %all_to_all.52 = bf16[8,88,512]{2,1,0:T(8,128)(2,1)S(1)} all-to-all(bf16[8,88,512]{2,1,0:T(8,128)(2,1)S(1)} %pad_maximum_fusion.1), channel_id=1, replica_groups=mesh['z'=8,'x'=4,'y'=8,'core'=2] {'z'}, dimensions={0} | all-to-all | bytes 1441792 | tf_op jit(solution)/shard_map/all_to_all | solution.py:129
  154.7 0.1 convert_reduce_fusion
  154.8 0.7 broadcast_in_dim.74
  155.5 5.4 %all-to-all-start.6 = ((bf16[4,56,512]{2,1,0:T(8,128)(2,1)}), bf16[4,56,512]{2,1,0:T(8,128)(2,1)S(1)}, u32[]{:S(2)}, u32[]{:S(2)}) async-start(bf16[4,56,512]{2,1,0:T(8,128)(2,1)} %broadcast_in_dim.74), calls=%async_computation.6 | async-start | bytes 458752 | tf_op jit(solution)/shard_map/all_to_all | solution.py:129
  160.9 0.0 all-gather.2.cloned.1.call-start
  161.0 4.4 %all-to-all-done.6 = bf16[4,56,512]{2,1,0:T(8,128)(2,1)S(1)} async-done(((bf16[4,56,512]{2,1,0:T(8,128)(2,1)}), bf16[4,56,512]{2,1,0:T(8,128)(2,1)S(1)}, u32[]{:S(2)}, u32[]{:S(2)}) %all-to-all-start.6) | async-done | bytes 229408 | tf_op jit(solution)/shard_map/all_to_all | solution.py:129
  165.3 0.7 copy-done.4
  166.0 0.0 all-gather.2.cloned.1.call-update
  166.1 12.9 %all_to_all.53 = f32[8,16,512]{2,1,0:T(8,128)S(1)} all-to-all(f32[8,16,512]{2,1,0:T(8,128)S(1)} %broadcast_in_dim.75), channel_id=1, replica_groups=mesh['z'=8,'x'=4,'y'=8,'core'=2] {'y'}, dimensions={0} | all-to-all | bytes 524288 | tf_op jit(solution)/shard_map/all_to_all | solution.py:129
  179.0 0.1 broadcast_in_dim.77
  179.1 13.3 %all_to_all.54 = f32[4,128,512]{2,1,0:T(8,128)S(1)} all-to-all(f32[4,128,512]{2,1,0:T(8,128)S(1)} %broadcast_in_dim.77), channel_id=1, replica_groups=mesh['z'=8,'x'=4,'y'=8,'core'=2] {'x'}, dimensions={0} | all-to-all | bytes 2097152 | tf_op jit(solution)/shard_map/all_to_all | solution.py:129
  192.4 19.1 %chol_inverse.1 = f32[512,512]{1,0:T(8,128)S(1)} custom-call(f32[512,512]{1,0:T(8,128)S(1)} %bitcast.65), custom_call_target="tpu_custom_call" | custom-call | flops 2000000000 | bytes 2097152 | tf_op jit(solution)/shard_map/chol_inverse/pallas_call | solution.py:116
  211.5 0.0 all-gather.2.cloned.1.call-done
  211.5 0.0 copy-start
  211.5 2.8 %fusion.16 = f32[1792,512]{1,0:T(8,128)S(1)} fusion(bf16[1792,512]{1,0:T(8,128)(2,1)} %all-gather.2.cloned.1.call-done, f32[512,512]{1,0:T(8,128)S(1)} %chol_inverse.1), kind=kOutput, calls=%fused_computation.30 | convolution fusion | flops 940048384 | bytes 6553600 | tf_op jit(solution)/shard_map/dot_general | solution.py:199
  214.4 0.0 copy-done
  214.4 1.3 multiply_reduce_fusion
  215.6 1.7 fusion.24
  217.4 1.9 fusion.23
  219.2 0.6 broadcast_in_dim.80
  219.8 3.3 %all-to-all-start.9 = ((f32[8,1,512]{2,1,0:T(1,128)}), f32[8,1,512]{2,1,0:T(1,128)S(1)}, u32[]{:S(2)}, u32[]{:S(2)}) async-start(f32[8,1,512]{2,1,0:T(1,128)} %broadcast_in_dim.80), calls=%async_computation.9 | async-start | bytes 32768 | tf_op jit(solution)/shard_map/all_to_all | solution.py:129
  223.2 0.0 copy-start.6
  223.2 0.0 copy-start.2
  223.2 0.0 copy-start.5
  223.2 3.3 %fusion.4 = bf16[1,256,1792]{2,1,0:T(8,128)(2,1)} fusion(bf16[1,256,1792]{2,1,0:T(8,128)(2,1)} %param.5, bf16[1,256,1792]{2,1,0:T(8,128)(2,1)} %param.6, bf16[1792,512]{1,0:T(8,128)(2,1)S(1)} %get-tuple-element.30, f32[]{:T(128)} %bitcast.3, f32[256,512]{1,0:T(8,128)} %fusion.23), kind=kOutput, calls=%fused_computation.9 | convolution fusion | flops 473104384 | bytes 5111812 | tf_op jit(solution)/shard_map/dot_general | solution.py:209
  226.6 4.3 %all-to-all-done.9 = f32[8,1,512]{2,1,0:T(1,128)S(1)} async-done(((f32[8,1,512]{2,1,0:T(1,128)}), f32[8,1,512]{2,1,0:T(1,128)S(1)}, u32[]{:S(2)}, u32[]{:S(2)}) %all-to-all-start.9) | async-done | bytes 16416 | tf_op jit(solution)/shard_map/all_to_all | solution.py:129
  230.9 0.0 copy-done.6
  230.9 0.7 multiply_bitcast_fusion
  231.6 0.0 copy-done.2
  231.6 1.6 fusion.3
  (13 shorter events, 0.2 us)
Async XLA Ops:
  7.2 12.1 %copy-start.1 = (bf16[1,256,1792]{2,1,0:T(8,128)(2,1)S(1)}, bf16[1,256,1792]{2,1,0:T(8,128)(2,1)}, u32[]{:S(2)}) copy-start(bf16[1,256,1792]{2,1,0:T(8,128)(2,1)} %param.5) | copy-start | bytes 2752516
  9.0 26.4 %all-to-all-start = ((bf16[8,56,512]{2,1,0:T(8,128)(2,1)}), bf16[8,56,512]{2,1,0:T(8,128)(2,1)S(1)}, u32[]{:S(2)}, u32[]{:S(2)}) async-start(bf16[8,56,512]{2,1,0:T(8,128)(2,1)} %broadcast_in_dim.33), calls=%async_computation | async-start | bytes 917504 | tf_op jit(solution)/shard_map/all_to_all | solution.py:129
  36.7 38.4 %all-to-all-start.1 = ((bf16[4,448,512]{2,1,0:T(8,128)(2,1)}), bf16[4,448,512]{2,1,0:T(8,128)(2,1)}, u32[]{:S(2)}, u32[]{:S(2)}) async-start(bf16[4,448,512]{2,1,0:T(8,128)(2,1)} %broadcast_in_dim.35), calls=%async_computation.1 | async-start | bytes 3670016 | tf_op jit(solution)/shard_map/all_to_all | solution.py:129
  75.2 1.8 copy-start.3
  96.2 16.7 %all-to-all-start.3 = ((f32[8,32,512]{2,1,0:T(8,128)}), f32[8,32,512]{2,1,0:T(8,128)S(1)}, u32[]{:S(2)}, u32[]{:S(2)}) async-start(f32[8,32,512]{2,1,0:T(8,128)} %broadcast_in_dim.72), calls=%async_computation.3 | async-start | bytes 1048576 | tf_op jit(solution)/shard_map/all_to_all | solution.py:129
  155.5 9.9 %all-to-all-start.6 = ((bf16[4,56,512]{2,1,0:T(8,128)(2,1)}), bf16[4,56,512]{2,1,0:T(8,128)(2,1)S(1)}, u32[]{:S(2)}, u32[]{:S(2)}) async-start(bf16[4,56,512]{2,1,0:T(8,128)(2,1)} %broadcast_in_dim.74), calls=%async_computation.6 | async-start | bytes 458752 | tf_op jit(solution)/shard_map/all_to_all | solution.py:129
  160.9 50.6 %all-gather.2.cloned.1.call-start = ((), (), s32[]{:S(2)}) async-start(), calls=%async_computation.10 | async-start | bytes 2064384 | tf_op jit(solution)/shard_map/all_gather | solution.py:193
  165.3 0.7 copy-start.4
  211.5 2.8 %copy-start = (bf16[1792,512]{1,0:T(8,128)(2,1)S(1)}, bf16[1792,512]{1,0:T(8,128)(2,1)}, u32[]{:S(2)}) copy-start(bf16[1792,512]{1,0:T(8,128)(2,1)} %all-gather.2.cloned.1.call-done) | copy-start | bytes 5505028
  219.8 11.0 %all-to-all-start.9 = ((f32[8,1,512]{2,1,0:T(1,128)}), f32[8,1,512]{2,1,0:T(1,128)S(1)}, u32[]{:S(2)}, u32[]{:S(2)}) async-start(f32[8,1,512]{2,1,0:T(1,128)} %broadcast_in_dim.80), calls=%async_computation.9 | async-start | bytes 32768 | tf_op jit(solution)/shard_map/all_to_all | solution.py:129
  223.2 7.7 %copy-start.6 = (f32[56,512]{1,0:T(8,128)S(1)}, f32[56,512]{1,0:T(8,128)}, u32[]{:S(2)}) copy-start(f32[56,512]{1,0:T(8,128)} %fusion.24) | copy-start | bytes 344068
  223.2 8.4 %copy-start.2 = (f32[256,512]{1,0:T(8,128)S(1)}, f32[256,512]{1,0:T(8,128)}, u32[]{:S(2)}) copy-start(f32[256,512]{1,0:T(8,128)} %fusion.23) | copy-start | bytes 1572868
  223.2 8.4 %copy-start.5 = (bf16[1,256,1792]{2,1,0:T(8,128)(2,1)S(1)}, bf16[1,256,1792]{2,1,0:T(8,128)(2,1)}, u32[]{:S(2)}) copy-start(bf16[1,256,1792]{2,1,0:T(8,128)(2,1)} %param.4) | copy-start | bytes 2752516
Sparse Core Ops, SparseCore 0:
  166.2 34.5 all-gather.1

commit v6 on v5

--- a/solution.py
+++ b/solution.py
@@ -154,10 +154,10 @@
 
     basis_z = spread(basis_low, "z").reshape(448, RANK)
     squares = jnp.full((1, 128), jnp.sum(grads * grads), f32)
-    squares = lax.psum(lax.psum(squares, "core"), "x")
+    squares = lax.psum(lax.psum(lax.psum(squares, "core"), "x"), "y")
     basis_z, squares = lax.optimization_barrier((basis_z, squares))
     basis_x = spread(basis_z, "x")
-    squares = lax.psum(lax.psum(squares, "y"), "z")
+    squares = lax.psum(squares, "z")
     basis_x, squares = lax.optimization_barrier((basis_x, squares))
     basis_all = natural(basis_x)
     square_total = squares[0, 0]

time: 242 us -> 244 us (level)
  waiting for transfers between devices: 26.4 us -> 21.9 us
  blocking collectives: 125 us -> 129 us
  starting transfers between devices: 27.4 us -> 30.4 us
    all_to_all x5, waiting for transfers between devices: 26.4 us -> 21.9 us  [swap(): return lax.all_to_all(x, axis, 0, 0, tiled=True)]
    all_to_all x5, starting transfers between devices: 27.4 us -> 30.4 us  [swap(): return lax.all_to_all(x, axis, 0, 0, tiled=True)]
  transfers between devices with their start and end apart: 6 -> 6, of which waited for: 4 -> 3; matrix products, arithmetic and copies ran while one was open for 2% -> 2% of each run, Pallas kernels for 8% -> 8%
where the time goes in v6:
time: 244 us; the launch traced here: 242 us
  blocking collectives  129 us (53%)
  starting transfers between devices  30.4 us (12%)
  waiting for transfers between devices  21.9 us (9%)
  Pallas kernels  19.1 us (8%)
  matrix products  15.6 us (6%)
  between operations  14.4 us (6%)
  local copies, waits for them, and re-layouts  7.95 us (3%)
  other arithmetic  3.78 us (2%)
    all_to_all x5, blocking collectives, swap(): return lax.all_to_all(x, axis, 0, 0, tiled=True)  84.1 us
    all_to_all x5, starting transfers between devices, swap(): return lax.all_to_all(x, axis, 0, 0, tiled=True)  30.4 us
    psum x3, blocking collectives, on_device(): squares = lax.psum(lax.psum(lax.psum(squares, 'core'), 'x'), 'y')  27.5 us
    all_to_all x5, waiting for transfers between devices, swap(): return lax.all_to_all(x, axis, 0, 0, tiled=True)  21.9 us
    pallas_call x1, Pallas kernels, chol_inverse(): pl.pallas_call(chol_inverse_kernel, out_shape=jax.ShapeDtypeStruct((RANK,...  19.1 us
    psum x1, blocking collectives, on_device(): squares = lax.psum(squares, 'z')  17.4 us
  transfers between devices with their start and end apart: 6, of which 3 were waited for; matrix products, arithmetic and copies ran while one was open for 2% of the time, Pallas kernels for 8%

profile of v6, /device:TPU:6, one launch (start us, length us, event | category | flops | bytes accessed | tf_op | source)
XLA Modules:
  0.0 242.3 jit_solution(11328174649852114953)
XLA Ops:
  7.2 0.0 copy-start.1
  7.2 1.0 convert_bitcast_fusion
  8.2 0.8 broadcast_in_dim.33
  9.0 10.3 %all-to-all-start = ((bf16[8,56,512]{2,1,0:T(8,128)(2,1)}), bf16[8,56,512]{2,1,0:T(8,128)(2,1)S(1)}, u32[]{:S(2)}, u32[]{:S(2)}) async-start(bf16[8,56,512]{2,1,0:T(8,128)(2,1)} %broadcast_in_dim.33), calls=%async_computation | async-start | bytes 917504 | tf_op jit(solution)/shard_map/all_to_all | solution.py:129
  19.3 0.0 copy-done.1
  19.3 1.1 fusion.5
  20.4 0.6 broadcast_in_dim.34
  21.0 2.5 %psum.28 = f32[1,128]{1,0:T(1,128)S(1)} all-reduce(f32[1,128]{1,0:T(1,128)S(1)} %broadcast_in_dim.34), channel_id=1, replica_groups=mesh['z'=8,'x'=4,'y'=8,'core'=2] {'core'}, use_global_device_ids=true, to_apply=%region_1.0 | all-reduce | flops 128 | bytes 1024 | tf_op jit(solution)/shard_map/psum | solution.py:157
  23.5 7.4 %psum.29 = f32[1,128]{1,0:T(1,128)S(1)} all-reduce(f32[1,128]{1,0:T(1,128)S(1)} %psum.28), channel_id=1, replica_groups=mesh['z'=8,'x'=4,'y'=8,'core'=2] {'x'}, use_global_device_ids=true, to_apply=%region_2.0 | all-reduce | flops 128 | bytes 1024 | tf_op jit(solution)/shard_map/psum | solution.py:157
  30.9 17.6 %psum.30 = f32[1,128]{1,0:T(1,128)S(1)} all-reduce(f32[1,128]{1,0:T(1,128)S(1)} %psum.29), channel_id=1, replica_groups=mesh['z'=8,'x'=4,'y'=8,'core'=2] {'y'}, use_global_device_ids=true, to_apply=%region_3.0 | all-reduce | flops 128 | bytes 1024 | tf_op jit(solution)/shard_map/psum | solution.py:157
  48.5 0.0 all-to-all-done
  48.5 1.4 broadcast_in_dim.35
  49.9 7.8 %all-to-all-start.1 = ((bf16[4,448,512]{2,1,0:T(8,128)(2,1)}), bf16[4,448,512]{2,1,0:T(8,128)(2,1)}, u32[]{:S(2)}, u32[]{:S(2)}) async-start(bf16[4,448,512]{2,1,0:T(8,128)(2,1)} %broadcast_in_dim.35), calls=%async_computation.1 | async-start | bytes 3670016 | tf_op jit(solution)/shard_map/all_to_all | solution.py:129
  57.8 17.4 %psum.31 = f32[1,128]{1,0:T(1,128)S(1)} all-reduce(f32[1,128]{1,0:T(1,128)S(1)} %psum.30), channel_id=1, replica_groups=mesh['z'=8,'x'=4,'y'=8,'core'=2] {'z'}, use_global_device_ids=true, to_apply=%region_4.0 | all-reduce | flops 128 | bytes 1024 | tf_op jit(solution)/shard_map/psum | solution.py:160
  75.1 0.0 all-to-all-done.1
  75.2 0.0 copy-start.3
  75.3 1.8 copy.16
  77.0 0.0 copy-done.3
  77.0 0.3 fusion.7
  77.3 0.6 fusion.21
  78.0 17.4 %all_to_all.50 = f32[8,32,512]{2,1,0:T(8,128)S(1)} all-to-all(f32[8,32,512]{2,1,0:T(8,128)S(1)} %fusion.21), channel_id=1, replica_groups=mesh['z'=8,'x'=4,'y'=8,'core'=2] {'y'}, dimensions={0} | all-to-all | bytes 1048576 | tf_op jit(solution)/shard_map/all_to_all | solution.py:129
  95.4 0.9 broadcast_in_dim.72
  96.3 3.5 %all-to-all-start.3 = ((f32[8,32,512]{2,1,0:T(8,128)}), f32[8,32,512]{2,1,0:T(8,128)S(1)}, u32[]{:S(2)}, u32[]{:S(2)}) async-start(f32[8,32,512]{2,1,0:T(8,128)} %broadcast_in_dim.72), calls=%async_computation.3 | async-start | bytes 1048576 | tf_op jit(solution)/shard_map/all_to_all | solution.py:129
  99.8 13.2 %all-to-all-done.3 = f32[8,32,512]{2,1,0:T(8,128)S(1)} async-done(((f32[8,32,512]{2,1,0:T(8,128)}), f32[8,32,512]{2,1,0:T(8,128)S(1)}, u32[]{:S(2)}, u32[]{:S(2)}) %all-to-all-start.3) | async-done | bytes 524320 | tf_op jit(solution)/shard_map/all_to_all | solution.py:129
  113.0 0.2 copy.18
  113.2 0.1 fusion.14
  113.3 0.7 fusion.10
  113.9 0.7 add_convert_fusion
  114.6 0.1 copy.17
  114.8 1.0 fusion.22
  115.8 0.1 pad_maximum_fusion
  116.0 18.4 %all_to_all.51 = bf16[4,480,512]{2,1,0:T(8,128)(2,1)S(1)} all-to-all(bf16[4,480,512]{2,1,0:T(8,128)(2,1)S(1)} %pad_maximum_fusion), channel_id=1, replica_groups=mesh['z'=8,'x'=4,'y'=8,'core'=2] {'x'}, dimensions={0} | all-to-all | bytes 3932160 | tf_op jit(solution)/shard_map/all_to_all | solution.py:129
  134.5 0.3 slice_reduce_fusion
  134.8 0.1 pad_maximum_fusion.1
  134.8 22.1 %all_to_all.52 = bf16[8,88,512]{2,1,0:T(8,128)(2,1)S(1)} all-to-all(bf16[8,88,512]{2,1,0:T(8,128)(2,1)S(1)} %pad_maximum_fusion.1), channel_id=1, replica_groups=mesh['z'=8,'x'=4,'y'=8,'core'=2] {'z'}, dimensions={0} | all-to-all | bytes 1441792 | tf_op jit(solution)/shard_map/all_to_all | solution.py:129
  156.9 0.1 convert_reduce_fusion
  157.0 0.7 broadcast_in_dim.74
  157.7 5.4 %all-to-all-start.6 = ((bf16[4,56,512]{2,1,0:T(8,128)(2,1)}), bf16[4,56,512]{2,1,0:T(8,128)(2,1)S(1)}, u32[]{:S(2)}, u32[]{:S(2)}) async-start(bf16[4,56,512]{2,1,0:T(8,128)(2,1)} %broadcast_in_dim.74), calls=%async_computation.6 | async-start | bytes 458752 | tf_op jit(solution)/shard_map/all_to_all | solution.py:129
  163.1 0.0 all-gather.2.cloned.1.call-start
  163.2 4.4 %all-to-all-done.6 = bf16[4,56,512]{2,1,0:T(8,128)(2,1)S(1)} async-done(((bf16[4,56,512]{2,1,0:T(8,128)(2,1)}), bf16[4,56,512]{2,1,0:T(8,128)(2,1)S(1)}, u32[]{:S(2)}, u32[]{:S(2)}) %all-to-all-start.6) | async-done | bytes 229408 | tf_op jit(solution)/shard_map/all_to_all | solution.py:129
  167.6 0.7 copy-done.4
  168.3 0.0 all-gather.2.cloned.1.call-update
  168.3 12.9 %all_to_all.53 = f32[8,16,512]{2,1,0:T(8,128)S(1)} all-to-all(f32[8,16,512]{2,1,0:T(8,128)S(1)} %broadcast_in_dim.75), channel_id=1, replica_groups=mesh['z'=8,'x'=4,'y'=8,'core'=2] {'y'}, dimensions={0} | all-to-all | bytes 524288 | tf_op jit(solution)/shard_map/all_to_all | solution.py:129
  181.2 0.1 broadcast_in_dim.77
  181.3 13.3 %all_to_all.54 = f32[4,128,512]{2,1,0:T(8,128)S(1)} all-to-all(f32[4,128,512]{2,1,0:T(8,128)S(1)} %broadcast_in_dim.77), channel_id=1, replica_groups=mesh['z'=8,'x'=4,'y'=8,'core'=2] {'x'}, dimensions={0} | all-to-all | bytes 2097152 | tf_op jit(solution)/shard_map/all_to_all | solution.py:129
  194.6 19.1 %chol_inverse.1 = f32[512,512]{1,0:T(8,128)S(1)} custom-call(f32[512,512]{1,0:T(8,128)S(1)} %bitcast.65), custom_call_target="tpu_custom_call" | custom-call | flops 2000000000 | bytes 2097152 | tf_op jit(solution)/shard_map/chol_inverse/pallas_call | solution.py:116
  213.7 0.0 all-gather.2.cloned.1.call-done
  213.8 0.0 copy-start
  213.8 2.8 %fusion.16 = f32[1792,512]{1,0:T(8,128)S(1)} fusion(bf16[1792,512]{1,0:T(8,128)(2,1)} %all-gather.2.cloned.1.call-done, f32[512,512]{1,0:T(8,128)S(1)} %chol_inverse.1), kind=kOutput, calls=%fused_computation.30 | convolution fusion | flops 940048384 | bytes 6553600 | tf_op jit(solution)/shard_map/dot_general | solution.py:199
  216.6 0.0 copy-done
  216.6 1.3 multiply_reduce_fusion
  217.9 1.7 fusion.24
  219.6 1.9 fusion.23
  221.5 0.6 broadcast_in_dim.80
  222.1 3.3 %all-to-all-start.9 = ((f32[8,1,512]{2,1,0:T(1,128)}), f32[8,1,512]{2,1,0:T(1,128)S(1)}, u32[]{:S(2)}, u32[]{:S(2)}) async-start(f32[8,1,512]{2,1,0:T(1,128)} %broadcast_in_dim.80), calls=%async_computation.9 | async-start | bytes 32768 | tf_op jit(solution)/shard_map/all_to_all | solution.py:129
  225.4 0.0 copy-start.6
  225.4 0.0 copy-start.2
  225.4 0.0 copy-start.5
  225.5 3.3 %fusion.4 = bf16[1,256,1792]{2,1,0:T(8,128)(2,1)} fusion(bf16[1,256,1792]{2,1,0:T(8,128)(2,1)} %param.5, bf16[1,256,1792]{2,1,0:T(8,128)(2,1)} %param.6, bf16[1792,512]{1,0:T(8,128)(2,1)S(1)} %get-tuple-element.30, f32[]{:T(128)} %bitcast.3, f32[256,512]{1,0:T(8,128)} %fusion.23), kind=kOutput, calls=%fused_computation.9 | convolution fusion | flops 473104384 | bytes 5111812 | tf_op jit(solution)/shard_map/dot_general | solution.py:209
  228.8 4.3 %all-to-all-done.9 = f32[8,1,512]{2,1,0:T(1,128)S(1)} async-done(((f32[8,1,512]{2,1,0:T(1,128)}), f32[8,1,512]{2,1,0:T(1,128)S(1)}, u32[]{:S(2)}, u32[]{:S(2)}) %all-to-all-start.9) | async-done | bytes 16416 | tf_op jit(solution)/shard_map/all_to_all | solution.py:129
  233.2 0.0 copy-done.6
  233.2 0.7 multiply_bitcast_fusion
  233.8 0.0 copy-done.2
  233.8 1.6 fusion.3
  (13 shorter events, 0.2 us)
Async XLA Ops:
  7.2 12.1 %copy-start.1 = (bf16[1,256,1792]{2,1,0:T(8,128)(2,1)S(1)}, bf16[1,256,1792]{2,1,0:T(8,128)(2,1)}, u32[]{:S(2)}) copy-start(bf16[1,256,1792]{2,1,0:T(8,128)(2,1)} %param.5) | copy-start | bytes 2752516
  9.0 39.6 %all-to-all-start = ((bf16[8,56,512]{2,1,0:T(8,128)(2,1)}), bf16[8,56,512]{2,1,0:T(8,128)(2,1)S(1)}, u32[]{:S(2)}, u32[]{:S(2)}) async-start(bf16[8,56,512]{2,1,0:T(8,128)(2,1)} %broadcast_in_dim.33), calls=%async_computation | async-start | bytes 917504 | tf_op jit(solution)/shard_map/all_to_all | solution.py:129
  49.9 25.2 %all-to-all-start.1 = ((bf16[4,448,512]{2,1,0:T(8,128)(2,1)}), bf16[4,448,512]{2,1,0:T(8,128)(2,1)}, u32[]{:S(2)}, u32[]{:S(2)}) async-start(bf16[4,448,512]{2,1,0:T(8,128)(2,1)} %broadcast_in_dim.35), calls=%async_computation.1 | async-start | bytes 3670016 | tf_op jit(solution)/shard_map/all_to_all | solution.py:129
  75.2 1.8 copy-start.3
  96.3 16.7 %all-to-all-start.3 = ((f32[8,32,512]{2,1,0:T(8,128)}), f32[8,32,512]{2,1,0:T(8,128)S(1)}, u32[]{:S(2)}, u32[]{:S(2)}) async-start(f32[8,32,512]{2,1,0:T(8,128)} %broadcast_in_dim.72), calls=%async_computation.3 | async-start | bytes 1048576 | tf_op jit(solution)/shard_map/all_to_all | solution.py:129
  157.7 9.9 %all-to-all-start.6 = ((bf16[4,56,512]{2,1,0:T(8,128)(2,1)}), bf16[4,56,512]{2,1,0:T(8,128)(2,1)S(1)}, u32[]{:S(2)}, u32[]{:S(2)}) async-start(bf16[4,56,512]{2,1,0:T(8,128)(2,1)} %broadcast_in_dim.74), calls=%async_computation.6 | async-start | bytes 458752 | tf_op jit(solution)/shard_map/all_to_all | solution.py:129
  163.1 50.6 %all-gather.2.cloned.1.call-start = ((), (), s32[]{:S(2)}) async-start(), calls=%async_computation.10 | async-start | bytes 2064384 | tf_op jit(solution)/shard_map/all_gather | solution.py:193
  167.6 0.7 copy-start.4
  213.8 2.8 %copy-start = (bf16[1792,512]{1,0:T(8,128)(2,1)S(1)}, bf16[1792,512]{1,0:T(8,128)(2,1)}, u32[]{:S(2)}) copy-start(bf16[1792,512]{1,0:T(8,128)(2,1)} %all-gather.2.cloned.1.call-done) | copy-start | bytes 5505028
  222.1 11.0 %all-to-all-start.9 = ((f32[8,1,512]{2,1,0:T(1,128)}), f32[8,1,512]{2,1,0:T(1,128)S(1)}, u32[]{:S(2)}, u32[]{:S(2)}) async-start(f32[8,1,512]{2,1,0:T(1,128)} %broadcast_in_dim.80), calls=%async_computation.9 | async-start | bytes 32768 | tf_op jit(solution)/shard_map/all_to_all | solution.py:129
  225.4 7.7 %copy-start.6 = (f32[56,512]{1,0:T(8,128)S(1)}, f32[56,512]{1,0:T(8,128)}, u32[]{:S(2)}) copy-start(f32[56,512]{1,0:T(8,128)} %fusion.24) | copy-start | bytes 344068
  225.4 8.4 %copy-start.2 = (f32[256,512]{1,0:T(8,128)S(1)}, f32[256,512]{1,0:T(8,128)}, u32[]{:S(2)}) copy-start(f32[256,512]{1,0:T(8,128)} %fusion.23) | copy-start | bytes 1572868
  225.4 8.4 %copy-start.5 = (bf16[1,256,1792]{2,1,0:T(8,128)(2,1)S(1)}, bf16[1,256,1792]{2,1,0:T(8,128)(2,1)}, u32[]{:S(2)}) copy-start(bf16[1,256,1792]{2,1,0:T(8,128)(2,1)} %param.4) | copy-start | bytes 2752516
Sparse Core Ops, SparseCore 0:
  168.4 34.5 all-gather.1
